TPU v7x, 32 devices: a whole 2x2x4 slice. The times are simulated.
32 devices in a mesh: rows: 8 (over z, x), cols: 4 (over y, core).
Axes of the slice: x: 2, y: 2, z: 4, core: 2. Of those that a mesh axis runs over, the one named last changes fastest.
Arguments:
- field: bfloat16 [1, 18432, 18432], P(None, 'rows', 'cols'), may hold values from -48 to 48
Outputs:
- spectra: float32 [1, 1152, 2304], P(None, ('rows', 'cols'))
All inputs are finite; a program needn't handle non-finite values.
Results may differ from a plain program's by a relative error of at most 0.0003.
The roundings to bfloat16 on the way count: a program that leaves them out, or rounds other values in their place, can miss the bound.
Values may be sent and summed in bfloat16 or wider, within the bound.
No kernel may reach another device: no remote copies, remote signals or barrier semaphores. Data moves between devices by JAX's collectives and lax.ppermute only.
A program may use at most 64 MiB of HBM per device.

v0:
```python
import functools
import math

import jax
import jax.numpy as jnp
import ml_dtypes
import numpy as np
from jax import lax
from jax.experimental import pallas as pl
from jax.experimental.pallas import tpu as pltpu
from jax.sharding import PartitionSpec as P

TAPS = 33
STRIDE = 8
REACH = TAPS // 2
GROUP_COLS = 1536
GROUP_OUTS = GROUP_COLS // STRIDE
LANES = 128
INNER = 256
ROW_MARGIN = 8
HALO_OUTS = 2


def ceil_to(value, step):
    return -(-value // step) * step


def split_host(table):
    high = table.astype(ml_dtypes.bfloat16)
    low = (table - high.astype(np.float64)).astype(ml_dtypes.bfloat16)
    return high, low


def taps_host():
    ids = np.arange(TAPS, dtype=np.float64)
    shaped = np.sinc((ids - REACH) / STRIDE) * (0.54 - 0.46 * np.cos(2 * np.pi * ids / (TAPS - 1)))
    return (shaped / shaped.sum()).astype(ml_dtypes.bfloat16)


def band_host(span_in, span_out, first_out):
    tap_ids = np.arange(span_in)[:, None] - STRIDE * (np.arange(span_out)[None, :] - first_out) + REACH
    table = taps_host()
    inside = (tap_ids >= 0) & (tap_ids < TAPS)
    return np.where(inside, table[np.clip(tap_ids, 0, TAPS - 1)], 0).astype(ml_dtypes.bfloat16)


def angles_host(left, right, length):
    reduced = (np.asarray(left)[:, None] * np.asarray(right)[None, :]) % length
    return 2 * np.pi * reduced / length


def split(value):
    high = value.astype(jnp.bfloat16)
    low = (value - high.astype(jnp.float32)).astype(jnp.bfloat16)
    return high, low


def dot(left, right):
    return jnp.dot(left, right, preferred_element_type=jnp.float32)


def dot_nt(left, right):
    return lax.dot_general(left, right, (((1,), (1,)), ((), ())), preferred_element_type=jnp.float32)


def cut_kernel(shape, field, band_cols, band_rows, row_weight, col_weight, out, total, tapered):
    groups, block_outs, fold, owners, own_rows = shape
    step = pl.program_id(0)

    @pl.when(step == 0)
    def _():
        total[...] = jnp.zeros_like(total)

    begin = pl.multiple_of(step * block_outs, 8)
    for group in range(groups):
        raw = field[0, :, group * GROUP_COLS : (group + 1) * GROUP_COLS]
        high, low = split(dot(raw, band_cols[...]))
        term = dot(band_rows[...], high) + dot(band_rows[...], low)
        total[group, pl.ds(begin, band_rows.shape[0]), :] += term

    @pl.when(step == pl.num_programs(0) - 1)
    def _():
        rows = owners * own_rows + 2 * ROW_MARGIN
        middle = jnp.concatenate([total[1, :rows, :], jnp.zeros((rows, LANES), jnp.float32)], axis=1)
        middle = pltpu.roll(middle, 64, 1)
        joined = [
            total[0, :rows, :LANES],
            total[0, :rows, LANES:] + middle[:, :LANES],
            middle[:, LANES : 2 * LANES],
            middle[:, 2 * LANES :] + total[2, :rows, :LANES],
            total[2, :rows, LANES:],
        ]
        for place, piece in enumerate(joined):
            lanes = slice(place * LANES, (place + 1) * LANES)
            tapered[place] = piece * row_weight[...] * col_weight[:, lanes]
        sub = lax.broadcasted_iota(jnp.int32, (8, LANES), 0)
        ahead, behind = ROW_MARGIN - 8, ROW_MARGIN + owners * own_rows
        for place in range(len(joined)):
            lanes = slice(place * LANES, (place + 1) * LANES)
            for owner in range(owners):
                begin_at = ROW_MARGIN + owner * own_rows
                for part in range(fold):
                    count = own_rows // fold
                    out[owner, part * count : (part + 1) * count, lanes] = tapered[
                        pl.ds(place, 1), pl.ds(begin_at + part, count, stride=fold), :
                    ][0]
                edge = (6, 7, 0, 1)[owner]
                first = ahead if owner < 2 else behind
                block = tapered[place, first : first + 8, :]
                block = jnp.where(sub == edge, block, 0.0)
                out[owner, own_rows : own_rows + 8, lanes] = pltpu.roll(block, (8 - edge) % 8, 0)


def cut_filter(field, row_weight, col_weight, owners, fold):
    _, raw_rows, raw_cols = field.shape
    block_rows = next(size for size in (256, 192, 128, 64) if raw_rows % size == 0)
    groups = raw_cols // GROUP_COLS
    block_outs = block_rows // STRIDE
    own_rows = raw_rows // STRIDE // owners
    span = block_outs + 2 * ROW_MARGIN
    band_cols = band_host(GROUP_COLS, 2 * LANES, HALO_OUTS)
    band_rows = band_host(block_rows, span, ROW_MARGIN).T
    out_cols = col_weight.shape[1]
    shape = (groups, block_outs, fold, owners, own_rows)
    return pl.pallas_call(
        functools.partial(cut_kernel, shape),
        grid=(raw_rows // block_rows,),
        out_shape=jax.ShapeDtypeStruct((owners, own_rows + 8, out_cols), jnp.float32),
        in_specs=[
            pl.BlockSpec((1, block_rows, raw_cols), lambda i: (0, i, 0)),
            pl.BlockSpec(band_cols.shape, lambda i: (0, 0)),
            pl.BlockSpec(band_rows.shape, lambda i: (0, 0)),
            pl.BlockSpec(row_weight.shape, lambda i: (0, 0)),
            pl.BlockSpec(col_weight.shape, lambda i: (0, 0)),
        ],
        out_specs=pl.BlockSpec((owners, own_rows + 8, out_cols), lambda i: (0, 0, 0)),
        scratch_shapes=[
            pltpu.VMEM((groups, raw_rows // STRIDE + 2 * ROW_MARGIN, 2 * LANES), jnp.float32),
            pltpu.VMEM((out_cols // LANES, raw_rows // STRIDE + 2 * ROW_MARGIN, LANES), jnp.float32),
        ],
        compiler_params=pltpu.CompilerParams(vmem_limit_bytes=48 * 2**20),
    )(field, jnp.asarray(band_cols), jnp.asarray(band_rows), row_weight, col_weight)


def column_kernel(shape, blocks, twiddle, high_table, low_table, out, joined, high_rows, low_rows):
    owners, rows, own_cols, fold = shape
    joined[...] = jnp.zeros_like(joined)
    width = blocks.shape[2]
    for owner in range(owners):
        first = LANES + own_cols * owner - HALO_OUTS
        block = jnp.concatenate([blocks[owner], jnp.zeros((rows, LANES), jnp.float32)], axis=1)
        base = first // LANES * LANES
        joined[:, base : base + width + LANES] += pltpu.roll(block, first - base, 1)
    points = [joined[:, LANES + INNER * i : LANES + INNER * (i + 1)] for i in range(fold)]
    half = fold // 2
    sums = [points[j] + points[fold - j] for j in range(1, half + 1)]
    differences = [points[j] - points[fold - j] for j in range(1, half + 1)]
    used = rows * fold
    if high_rows.shape[0] > used:
        rest = jnp.zeros((high_rows.shape[0] - used, 2 * INNER), jnp.bfloat16)
        high_rows[used:, :] = rest
        low_rows[used:, :] = rest

    def keep(freq, real, imag):
        for side, value in enumerate((real, imag)):
            high, low = split(value)
            place = (slice(freq * rows, (freq + 1) * rows), slice(side * INNER, (side + 1) * INNER))
            high_rows[place] = high
            low_rows[place] = low

    def turned(freq, real, imag):
        tc = twiddle[freq : freq + 1, :INNER]
        ts = twiddle[freq : freq + 1, INNER:]
        keep(freq, real * tc + imag * ts, imag * tc - real * ts)

    keep(0, functools.reduce(jnp.add, sums, points[0]), jnp.zeros((rows, INNER), jnp.float32))
    for freq in range(1, half + 1):
        real, imag = points[0], None
        for j in range(1, half + 1):
            angle = 2 * math.pi * ((j * freq) % fold) / fold
            real = real + math.cos(angle) * sums[j - 1]
            term = -math.sin(angle) * differences[j - 1]
            imag = term if imag is None else imag + term
        turned(freq, real, imag)
        turned(fold - freq, real, -imag)
    result = dot_nt(high_table[...], high_rows[...])
    result += dot_nt(high_table[...], low_rows[...])
    result += dot_nt(low_table[...], high_rows[...])
    out[...] = result.reshape(out.shape)


def column_transform(blocks, length, devices):
    owners, rows, width = blocks.shape
    own_cols = length // owners
    fold = length // INNER
    kept = INNER // 2
    per_device = kept // devices
    angle = angles_host(np.arange(fold), np.arange(INNER), length)
    twiddle = np.concatenate([np.cos(angle), np.sin(angle)], axis=1).astype(np.float32)
    angle = angles_host(np.arange(kept), np.arange(INNER), INNER)
    table = np.stack(
        [
            np.concatenate([np.cos(angle), np.sin(angle)], axis=1),
            np.concatenate([-np.sin(angle), np.cos(angle)], axis=1),
        ]
    )
    table = table.reshape(2, devices, per_device, 2 * INNER).transpose(1, 0, 2, 3).reshape(INNER, 2 * INNER)
    high_table, low_table = split_host(table)
    lanes = ceil_to(fold * rows, LANES)
    return pl.pallas_call(
        functools.partial(column_kernel, (owners, rows, own_cols, fold)),
        out_shape=jax.ShapeDtypeStruct((devices, 2 * per_device, lanes), jnp.float32),
        scratch_shapes=[
            pltpu.VMEM((rows, length + 2 * LANES), jnp.float32),
            pltpu.VMEM((lanes, 2 * INNER), jnp.bfloat16),
            pltpu.VMEM((lanes, 2 * INNER), jnp.bfloat16),
        ],
        compiler_params=pltpu.CompilerParams(vmem_limit_bytes=48 * 2**20),
    )(blocks, jnp.asarray(twiddle), jnp.asarray(high_table), jnp.asarray(low_table))


def row_kernel(shape, arrived, twiddle, high_table, low_table, out, spread, folded):
    length, fold, step, parts, scale = shape
    devices, packed, width = arrived.shape
    per_device = packed // 2
    slots = LANES // step
    lane = lax.broadcasted_iota(jnp.int32, (packed, LANES), 1) // step
    sign = jnp.where(lax.broadcasted_iota(jnp.int32, (packed, INNER), 0) < per_device, 1.0, -1.0)

    for column in range(width // LANES):
        for half in range(devices // slots):
            tiles = [
                arrived[half * slots + g, :, column * LANES : (column + 1) * LANES] for g in range(slots)
            ]
            bit = 1
            while bit < slots:
                upper = (lane & bit) != 0
                for g in range(slots):
                    if g & bit:
                        continue
                    a, b = tiles[g], tiles[g + bit]
                    tiles[g] = jnp.where(upper, pltpu.roll(b, bit * step, 1), a)
                    tiles[g + bit] = jnp.where(upper, b, pltpu.roll(a, LANES - bit * step, 1))
                bit *= 2
            for g in range(slots):
                q = column * slots + g
                if q < fold * parts:
                    spread[q, :, half * LANES : (half + 1) * LANES] = tiles[g]

    def quarter(value):
        return pltpu.roll(value, per_device, 0) * sign

    place = lax.broadcasted_iota(jnp.int32, (packed, INNER), 1)
    for freq in range(fold):
        halo = spread[freq * parts + fold]
        run = 4 * step
        extra = {}
        for owner, (target, shift) in enumerate(
            ((fold - 2, -1), (fold - 1, -1 - step), (0, 2 * step), (1, step))
        ):
            only = jnp.where(place % run == owner * step, halo, 0.0)
            moved = pltpu.roll(only, shift % INNER, 1)
            extra[target] = extra[target] + moved if target in extra else moved
        for point in range(fold):
            value = spread[freq * parts + point]
            if point in extra:
                value = value + extra[point]
            folded[(point * fold + freq) * packed : (point * fold + freq + 1) * packed, :] = value

    high, low = split(folded[...])
    result = dot(high, high_table[...]) + dot(low, high_table[...]) + dot(high, low_table[...])
    for freq in range(fold):
        points = []
        for point in range(fold):
            begin = (point * fold + freq) * packed
            rows = slice(begin, begin + packed)
            value = result[rows, :INNER] + quarter(result[rows, INNER:])
            if point:
                tc = twiddle[point : point + 1, :INNER]
                ts = twiddle[point : point + 1, INNER:]
                value = value * tc + quarter(value) * ts
            points.append(value)
        half = fold // 2
        sums = [points[j] + points[fold - j] for j in range(1, half + 1)]
        differences = [quarter(points[j] - points[fold - j]) for j in range(1, half + 1)]

        def keep(index, value):
            power = value * value
            power = (power + pltpu.roll(power, per_device, 0)) * scale
            for own in range(per_device):
                row = own * fold + freq
                out[0, row : row + 1, index * INNER : (index + 1) * INNER] = power[own : own + 1]

        keep(0, functools.reduce(jnp.add, sums, points[0]))
        for index in range(1, half + 1):
            even, odd = points[0], None
            for j in range(1, half + 1):
                angle = 2 * math.pi * ((j * index) % fold) / fold
                even = even + math.cos(angle) * sums[j - 1]
                term = math.sin(angle) * differences[j - 1]
                odd = term if odd is None else odd + term
            keep(index, even + odd)
            keep(fold - index, even - odd)


def row_transform(arrived, length, rows):
    devices, packed, width = arrived.shape
    fold = length // INNER
    step = length // fold // devices
    angle = angles_host(np.arange(fold), np.arange(INNER), length)
    twiddle = np.concatenate([np.cos(angle), np.sin(angle)], axis=1).astype(np.float32)
    angle = angles_host(np.arange(INNER), np.arange(INNER), INNER)
    high_table, low_table = split_host(np.concatenate([np.cos(angle), np.sin(angle)], axis=1))
    parts = rows // step
    shape = (length, fold, step, parts, STRIDE / (length * length))
    return pl.pallas_call(
        functools.partial(row_kernel, shape),
        out_shape=jax.ShapeDtypeStruct((1, fold * packed // 2, length), jnp.float32),
        scratch_shapes=[
            pltpu.VMEM((fold * parts, packed, INNER), jnp.float32),
            pltpu.VMEM((fold * fold * packed, INNER), jnp.float32),
        ],
        compiler_params=pltpu.CompilerParams(vmem_limit_bytes=48 * 2**20),
    )(arrived, jnp.asarray(twiddle), jnp.asarray(high_table), jnp.asarray(low_table))


def taper(ids, length):
    weight = 0.5 - 0.5 * jnp.cos(2 * jnp.pi * ids.astype(jnp.float32) / length)
    return jnp.where((ids >= 0) & (ids < length), weight, 0.0)


def local(field):
    owners = lax.axis_size("cols")
    devices = lax.axis_size("rows") * owners
    own_rows = field.shape[1] // STRIDE
    own_cols = field.shape[2] // STRIDE
    length = own_rows * lax.axis_size("rows")
    fold = length // INNER
    lanes = ceil_to(own_cols + 2 * HALO_OUTS, LANES)
    row_ids = lax.axis_index("rows") * own_rows + jnp.arange(-ROW_MARGIN, own_rows + ROW_MARGIN)
    col_ids = lax.axis_index("cols") * own_cols + jnp.arange(-HALO_OUTS, lanes - HALO_OUTS)
    row_weight = taper(row_ids, length)[:, None]
    col_weight = taper(col_ids, length)[None, :]
    tapered = cut_filter(field, row_weight, col_weight, owners, fold)
    grouped = lax.all_to_all(tapered, "cols", split_axis=0, concat_axis=0, tiled=True)
    partial = column_transform(grouped, length, devices)
    arrived = lax.all_to_all(partial, ("rows", "cols"), split_axis=0, concat_axis=0, tiled=True)
    return row_transform(arrived, length, grouped.shape[1])


def solution(mesh):
    return jax.shard_map(
        local,
        mesh=mesh,
        in_specs=(P(None, "rows", "cols"),),
        out_specs=P(None, ("rows", "cols"), None),
        check_vma=False,
    )
```

profile of v0, /device:TPU:0, one launch (start us, length us, event | category | flops | bytes accessed | tf_op | source)
XLA Modules:
  0.0 66.3 jit_solution(4617165919196646443)
XLA Ops:
  0.0 0.0 copy-start.5
  0.0 0.1 and_select_fusion.col_weight
  0.1 0.6 subtract_select_fusion.row_weight
  0.7 0.0 copy-start
  0.7 1.1 %copy-done = bf16[1536,256]{1,0:T(8,128)(2,1)S(1)} copy-done((bf16[1536,256]{1,0:T(8,128)(2,1)S(1)}, bf16[1536,256]{1,0:T(8,128)(2,1)}, u32[]{:S(2)}) %copy-start) | copy-done | bytes 786456
  1.8 0.0 copy-start.6
  1.8 0.7 %copy-done.6 = bf16[48,256]{1,0:T(8,128)(2,1)S(1)} copy-done((bf16[48,256]{1,0:T(8,128)(2,1)S(1)}, bf16[48,256]{1,0:T(8,128)(2,1)}, u32[]{:S(2)}) %copy-start.6) | copy-done | bytes 24600
  2.5 0.0 copy-start.1
  2.5 0.0 copy-start.2
  2.5 0.0 copy-start.3
  2.6 0.0 copy-start.4
  2.6 18.2 %shard_map.91 = f32[4,80,640]{2,1,0:T(8,128)S(1)} custom-call(bf16[1,2304,4608]{2,1,0:T(8,128)(2,1)} %field.1, bf16[1536,256]{1,0:T(8,128)(2,1)S(1)} %copy-done, bf16[48,256]{1,0:T(8,128)(2,1)S(1)} %copy-done.6, f32[304,1]{1,0:T(8,128)S(1)} %subtract_select_fusion.row_weight, f32[1,640]{1,0:T(1,128)S(1)} %and_select_fusion.col_weight), custom_call_target="tpu_custom_call" | custom-call | tf_op jit(solution)/shard_map/pallas_call | solution.py:125
  20.8 16.0 %all_to_all.10.blocks = f32[4,80,640]{2,1,0:T(8,128)S(1)} all-to-all(f32[4,80,640]{2,1,0:T(8,128)S(1)} %shard_map.91), channel_id=1, replica_groups=mesh['rows'=8,'cols'=4] {'cols'}, dimensions={0} | all-to-all | bytes 1638400 | tf_op jit(solution)/shard_map/all_to_all | solution.py:345
  36.9 0.0 copy-done.5
  36.9 0.0 copy-done.1
  36.9 0.0 copy-done.2
  36.9 1.2 %shard_map.92 = f32[32,8,768]{2,1,0:T(8,128)S(1)} custom-call(f32[4,80,640]{2,1,0:T(8,128)S(1)} %all_to_all.10.blocks, f32[9,512]{1,0:T(8,128)S(1)} %copy-done.5, bf16[256,512]{1,0:T(8,128)(2,1)S(1)} %copy-done.2, bf16[256,512]{1,0:T(8,128)(2,1)S(1)} %copy-done.1), custom_call_target="tpu_custom_call" | custom-call | tf_op jit(solution)/shard_map/pallas_call | solution.py:210
  38.1 25.3 %all_to_all.11.arrived = f32[32,8,768]{2,1,0:T(8,128)S(1)} all-to-all(f32[32,8,768]{2,1,0:T(8,128)S(1)} %shard_map.92), channel_id=1, replica_groups=mesh['rows'=8,'cols'=4] {'rows','cols'}, dimensions={0} | all-to-all | bytes 1572864 | tf_op jit(solution)/shard_map/all_to_all | solution.py:347
  63.4 0.0 copy-done.3
  63.4 0.0 copy-done.4
  63.4 1.9 %shard_map.93 = f32[1,36,2304]{2,1,0:T(8,128)S(1)} custom-call(f32[32,8,768]{2,1,0:T(8,128)S(1)} %all_to_all.11.arrived, f32[9,512]{1,0:T(8,128)S(1)} %copy-done.5, bf16[256,512]{1,0:T(8,128)(2,1)S(1)} %copy-done.4, bf16[256,512]{1,0:T(8,128)(2,1)S(1)} %copy-done.3), custom_call_target="tpu_custom_call" | custom-call | tf_op jit(solution)/shard_map/pallas_call | solution.py:316
  65.3 1.1 %copy.12 = f32[1,36,2304]{2,0,1:T(1,128)} copy(f32[1,36,2304]{2,1,0:T(8,128)S(1)} %shard_map.93) | data formatting | bytes 663552 | tf_op jit(solution)/shard_map/pallas_call | solution.py:316
Async XLA Ops:
  0.0 36.9 %copy-start.5 = (f32[9,512]{1,0:T(8,128)S(1)}, f32[9,512]{1,0:T(8,128)}, u32[]{:S(2)}) copy-start(f32[9,512]{1,0:T(8,128)} %constant.53.clone.twiddle) | copy-start | bytes 55300
  0.7 1.1 %copy-start = (bf16[1536,256]{1,0:T(8,128)(2,1)S(1)}, bf16[1536,256]{1,0:T(8,128)(2,1)}, u32[]{:S(2)}) copy-start(bf16[1536,256]{1,0:T(8,128)(2,1)} %constant.51.clone.band_cols) | copy-start | bytes 2359300
  1.8 0.7 %copy-start.6 = (bf16[48,256]{1,0:T(8,128)(2,1)S(1)}, bf16[48,256]{1,0:T(8,128)(2,1)}, u32[]{:S(2)}) copy-start(bf16[48,256]{1,0:T(8,128)(2,1)} %constant.52.clone.band_rows) | copy-start | bytes 73732
  2.5 34.3 %copy-start.1 = (bf16[256,512]{1,0:T(8,128)(2,1)S(1)}, bf16[256,512]{1,0:T(8,128)(2,1)}, u32[]{:S(2)}) copy-start(bf16[256,512]{1,0:T(8,128)(2,1)} %constant.55.clone.low_table) | copy-start | bytes 786436
  2.5 34.3 %copy-start.2 = (bf16[256,512]{1,0:T(8,128)(2,1)S(1)}, bf16[256,512]{1,0:T(8,128)(2,1)}, u32[]{:S(2)}) copy-start(bf16[256,512]{1,0:T(8,128)(2,1)} %constant.54.clone.high_table) | copy-start | bytes 786436
  2.5 60.8 %copy-start.3 = (bf16[256,512]{1,0:T(8,128)(2,1)S(1)}, bf16[256,512]{1,0:T(8,128)(2,1)}, u32[]{:S(2)}) copy-start(bf16[256,512]{1,0:T(8,128)(2,1)} %constant.57.clone.low_table) | copy-start | bytes 786436
  2.6 60.8 %copy-start.4 = (bf16[256,512]{1,0:T(8,128)(2,1)S(1)}, bf16[256,512]{1,0:T(8,128)(2,1)}, u32[]{:S(2)}) copy-start(bf16[256,512]{1,0:T(8,128)(2,1)} %constant.56.clone.high_table) | copy-start | bytes 786436
where the time goes:
time: 66.6 us; the launch traced here: 66.3 us
  blocking collectives  41.4 us (62%)
  Pallas kernels  21.3 us (32%)
  local copies, waits for them, and re-layouts  2.95 us (4%)
    all_to_all x1, blocking collectives, local(): lax.all_to_all(partial, ('rows', 'cols'), split_axis=0, concat_axis=0, ti...  25.3 us
    pallas_call x1, Pallas kernels, cut_filter(): pl.pallas_call(functools.partial(cut_kernel, shape), grid=(raw_rows // bl...  18.2 us
    all_to_all x1, blocking collectives, local(): lax.all_to_all(tapered, 'cols', split_axis=0, concat_axis=0, tiled=True)  16 us
    unnamed x14, local copies, waits for them, and re-layouts  1.88 us
    pallas_call x1, Pallas kernels, row_transform(): pl.pallas_call(functools.partial(row_kernel, shape), out_shape=jax.ShapeD...  1.88 us

commit v1 on v0

v1 whole, which is shorter than its diff:
```python
import functools
import math

import jax
import jax.numpy as jnp
import ml_dtypes
import numpy as np
from jax import lax
from jax.experimental import pallas as pl
from jax.experimental.pallas import tpu as pltpu
from jax.sharding import PartitionSpec as P

TAPS = 33
STRIDE = 8
REACH = TAPS // 2
GROUP_COLS = 1536
GROUP_OUTS = GROUP_COLS // STRIDE
LANES = 128
INNER = 256
COMPAND = 1023.0
LEVELS = 240
NONE_CODE = 2.0 ** -(LEVELS // 2)
ROW_MARGIN = 8
HALO_OUTS = 2


def ceil_to(value, step):
    return -(-value // step) * step


def split_host(table):
    high = table.astype(ml_dtypes.bfloat16)
    low = (table - high.astype(np.float64)).astype(ml_dtypes.bfloat16)
    return high, low


def taps_host():
    ids = np.arange(TAPS, dtype=np.float64)
    shaped = np.sinc((ids - REACH) / STRIDE) * (0.54 - 0.46 * np.cos(2 * np.pi * ids / (TAPS - 1)))
    return (shaped / shaped.sum()).astype(ml_dtypes.bfloat16)


def band(taps, tap_ids):
    table = jnp.zeros(tap_ids.shape, jnp.float32)
    for tap_id, tap in enumerate(taps):
        table = jnp.where(tap_ids == tap_id, tap, table)
    return table


def angles_host(left, right, length):
    reduced = (np.asarray(left)[:, None] * np.asarray(right)[None, :]) % length
    return 2 * np.pi * reduced / length


def taper_host(length):
    return (0.5 - 0.5 * np.cos(2 * np.pi * np.arange(length) / length)).astype(np.float32)


def split(value):
    high = value.astype(jnp.bfloat16)
    low = (value - high.astype(jnp.float32)).astype(jnp.bfloat16)
    return high, low


def row_scale(*arrays):
    peak = functools.reduce(jnp.maximum, [jnp.abs(array) for array in arrays])
    peak = jnp.max(peak, axis=-1, keepdims=True)
    return (peak * 1.01 + 1e-30).astype(jnp.bfloat16).astype(jnp.float32)


def encode(value, scale):
    level = jnp.log(1.0 + jnp.abs(value) * (COMPAND / scale)) * (LEVELS / math.log(1.001 * COMPAND))
    whole = jnp.floor(level)
    code = (1.0 + (level - whole)) * jnp.exp2(whole - LEVELS / 2)
    return jnp.where(value < 0, -code, code)


def decode(code, scale):
    size = jnp.abs(code)
    whole = jnp.floor(jnp.log2(size) + 0.0028)
    level = whole + (LEVELS / 2 - 1.0) + size * jnp.exp2(-whole)
    value = (jnp.exp(level * (math.log(1.001 * COMPAND) / LEVELS)) - 1.0) * (scale / COMPAND)
    return jnp.where(code < 0, -value, value)


def dot(left, right):
    return jnp.dot(left, right, preferred_element_type=jnp.float32)


def dot_nt(left, right):
    return lax.dot_general(left, right, (((1,), (1,)), ((), ())), preferred_element_type=jnp.float32)


def cut_kernel(shape, field, out, raw, arrived, band_rows, band_cols, total, cut, ordered):
    taps, chunks, groups, block_outs, fold, owners, own_rows = shape
    block_rows = raw.shape[1]

    def copy(chunk):
        rows = pl.ds(pl.multiple_of(chunk * block_rows, block_rows), block_rows)
        return pltpu.make_async_copy(field.at[0, rows, :], raw.at[chunk], arrived.at[chunk])

    for chunk in range(chunks):
        copy(chunk).start()
    total[...] = jnp.zeros_like(total)
    ids = lax.broadcasted_iota(jnp.int32, band_rows.shape, 1)
    ids = ids - STRIDE * (lax.broadcasted_iota(jnp.int32, band_rows.shape, 0) - ROW_MARGIN) + REACH
    band_rows[...] = band(taps, ids).astype(jnp.bfloat16)
    shape_8 = (8, band_cols.shape[1])
    ids = lax.broadcasted_iota(jnp.int32, shape_8, 0)
    ids = ids - STRIDE * (lax.broadcasted_iota(jnp.int32, shape_8, 1) - HALO_OUTS) + REACH
    initial = band(taps, ids)
    for pair in range(GROUP_COLS // 16):
        both = [pltpu.roll(initial, move, 1) if move else initial for move in (2 * pair, 2 * pair + 1)]
        band_cols[16 * pair : 16 * pair + 16, :] = jnp.concatenate(both, axis=0).astype(jnp.bfloat16)

    def step(chunk, carry):
        copy(chunk).wait()
        stacked = jnp.concatenate(
            [raw[chunk, :, group * GROUP_COLS : (group + 1) * GROUP_COLS] for group in range(groups)], axis=0
        )
        high, low = split(dot(stacked, band_cols[...]))
        rows = pl.ds(pl.multiple_of(chunk * block_outs, 8), band_rows.shape[0])
        for group in range(groups):
            own = slice(group * block_rows, (group + 1) * block_rows)
            term = dot(band_rows[...], high[own]) + dot(band_rows[...], low[own])
            total[group, rows, :] += term
        return carry

    lax.fori_loop(0, chunks, step, 0)
    count_rows = owners * own_rows + 2 * ROW_MARGIN
    middle = jnp.concatenate([total[1], jnp.zeros((count_rows, LANES), jnp.float32)], axis=1)
    middle = pltpu.roll(middle, 64, 1)
    cut[0] = total[0, :, :LANES]
    cut[1] = total[0, :, LANES:] + middle[:, :LANES]
    cut[2] = middle[:, LANES : 2 * LANES]
    cut[3] = middle[:, 2 * LANES :] + total[2, :, :LANES]
    cut[4] = total[2, :, LANES:]
    places = cut.shape[0]
    scale = row_scale(*[cut[place] for place in range(places)])
    last = lax.broadcasted_iota(jnp.int32, (count_rows, LANES), 1) == LANES - 1
    for place in range(places):
        code = encode(cut[place], scale)
        cut[place] = jnp.where(last, scale, code) if place == places - 1 else code
    used = own_rows + 8
    sub = lax.broadcasted_iota(jnp.int32, (8, LANES), 0)
    behind = ROW_MARGIN + owners * own_rows
    if ordered.shape[0] > used:
        ordered[used:, :] = jnp.full((ordered.shape[0] - used, ordered.shape[1]), NONE_CODE, jnp.float32)
    for owner in range(owners):
        begin_at = ROW_MARGIN + owner * own_rows
        count = own_rows // fold
        edge = (ROW_MARGIN - 2, ROW_MARGIN - 1, 0, 1)[owner]
        first = 0 if owner < 2 else behind
        for place in range(places):
            lanes = slice(place * LANES, (place + 1) * LANES)
            for part in range(fold):
                picked = cut[pl.ds(place, 1), pl.ds(begin_at + part, count, stride=fold), :]
                ordered[part * count : (part + 1) * count, lanes] = picked[0]
            block = pltpu.roll(cut[place, first : first + 8, :], (8 - edge) % 8, 0)
            ordered[own_rows:used, lanes] = jnp.where(sub == 0, block, NONE_CODE)
        out[owner] = ordered[...].astype(jnp.bfloat16)


def cut_filter(field, owners, fold):
    _, raw_rows, raw_cols = field.shape
    block_rows = next(size for size in (256, 192, 128, 64) if raw_rows % size == 0)
    chunks = raw_rows // block_rows
    groups = raw_cols // GROUP_COLS
    block_outs = block_rows // STRIDE
    own_rows = raw_rows // STRIDE // owners
    span = block_outs + 2 * ROW_MARGIN
    count_rows = raw_rows // STRIDE + 2 * ROW_MARGIN
    out_cols = ceil_to(raw_cols // STRIDE + 2 * HALO_OUTS, LANES)
    taps = [float(tap) for tap in taps_host()]
    shape = (taps, chunks, groups, block_outs, fold, owners, own_rows)
    out_rows = ceil_to(own_rows + 8, 16)
    return pl.pallas_call(
        functools.partial(cut_kernel, shape),
        out_shape=jax.ShapeDtypeStruct((owners, out_rows, out_cols), jnp.bfloat16),
        in_specs=[pl.BlockSpec(memory_space=pl.ANY)],
        out_specs=pl.BlockSpec(memory_space=pltpu.VMEM),
        scratch_shapes=[
            pltpu.VMEM((chunks, block_rows, raw_cols), jnp.bfloat16),
            pltpu.SemaphoreType.DMA((chunks,)),
            pltpu.VMEM((span, block_rows), jnp.bfloat16),
            pltpu.VMEM((GROUP_COLS, 2 * LANES), jnp.bfloat16),
            pltpu.VMEM((groups, count_rows, 2 * LANES), jnp.float32),
            pltpu.VMEM((out_cols // LANES, count_rows, LANES), jnp.float32),
            pltpu.VMEM((out_rows, out_cols), jnp.float32),
        ],
        compiler_params=pltpu.CompilerParams(vmem_limit_bytes=40 * 2**20),
    )(field)


def column_kernel(shape, blocks, weight, twiddle, high_table, low_table, out, joined, high_rows, low_rows):
    owners, rows, own_cols, fold = shape
    joined[...] = jnp.zeros_like(joined)
    width = blocks.shape[2]
    inside = lax.broadcasted_iota(jnp.int32, (rows, width), 1) < own_cols + 2 * HALO_OUTS
    for owner in range(owners):
        first = LANES + own_cols * owner - HALO_OUTS
        code = blocks[owner].astype(jnp.float32)
        value = decode(code, code[:, width - 1 :])
        value = jnp.where(inside, value, 0.0)
        block = jnp.concatenate([value, jnp.zeros((rows, LANES), jnp.float32)], axis=1)
        base = first // LANES * LANES
        joined[:, base : base + width + LANES] += pltpu.roll(block, first - base, 1)
    points = [
        joined[:, LANES + INNER * i : LANES + INNER * (i + 1)] * weight[:, INNER * i : INNER * (i + 1)]
        for i in range(fold)
    ]
    half = fold // 2
    sums = [points[j] + points[fold - j] for j in range(1, half + 1)]
    differences = [points[j] - points[fold - j] for j in range(1, half + 1)]
    used = rows * fold
    if high_rows.shape[0] > used:
        rest = jnp.zeros((high_rows.shape[0] - used, 2 * INNER), jnp.bfloat16)
        high_rows[used:, :] = rest
        low_rows[used:, :] = rest

    def keep(freq, real, imag):
        for side, value in enumerate((real, imag)):
            high, low = split(value)
            place = (slice(freq * rows, (freq + 1) * rows), slice(side * INNER, (side + 1) * INNER))
            high_rows[place] = high
            low_rows[place] = low

    def turned(freq, real, imag):
        tc = twiddle[freq : freq + 1, :INNER]
        ts = twiddle[freq : freq + 1, INNER:]
        keep(freq, real * tc + imag * ts, imag * tc - real * ts)

    keep(0, functools.reduce(jnp.add, sums, points[0]), jnp.zeros((rows, INNER), jnp.float32))
    for freq in range(1, half + 1):
        real, imag = points[0], None
        for j in range(1, half + 1):
            angle = 2 * math.pi * ((j * freq) % fold) / fold
            real = real + math.cos(angle) * sums[j - 1]
            term = -math.sin(angle) * differences[j - 1]
            imag = term if imag is None else imag + term
        turned(freq, real, imag)
        turned(fold - freq, real, -imag)
    result = dot_nt(high_table[...], high_rows[...])
    result += dot_nt(high_table[...], low_rows[...])
    result += dot_nt(low_table[...], high_rows[...])
    scale = row_scale(result)
    code = encode(result, scale)
    lane = lax.broadcasted_iota(jnp.int32, code.shape, 1)
    code = jnp.where(lane == code.shape[1] - 1, scale, code)
    devices, tall, wide = out.shape
    pieces = code.shape[1] // wide
    code = code.reshape(devices, tall // pieces, code.shape[1])
    code = [code[:, :, piece * wide : (piece + 1) * wide] for piece in range(pieces)]
    out[...] = jnp.concatenate(code, axis=1).astype(jnp.bfloat16)


def column_transform(blocks, length, devices):
    owners, rows, width = blocks.shape
    own_cols = length // owners
    fold = length // INNER
    kept = INNER // 2
    per_device = kept // devices
    angle = angles_host(np.arange(fold), np.arange(INNER), length)
    twiddle = np.concatenate([np.cos(angle), np.sin(angle)], axis=1).astype(np.float32)
    angle = angles_host(np.arange(kept), np.arange(INNER), INNER)
    table = np.stack(
        [
            np.concatenate([np.cos(angle), np.sin(angle)], axis=1),
            np.concatenate([-np.sin(angle), np.cos(angle)], axis=1),
        ]
    )
    table = table.reshape(2, devices, per_device, 2 * INNER).transpose(1, 0, 2, 3).reshape(INNER, 2 * INNER)
    high_table, low_table = split_host(table)
    pieces = max(16 // (2 * per_device), 1)
    lanes = ceil_to(fold * rows + 1, pieces * LANES)
    return pl.pallas_call(
        functools.partial(column_kernel, (owners, rows, own_cols, fold)),
        out_shape=jax.ShapeDtypeStruct((devices, pieces * 2 * per_device, lanes // pieces), jnp.bfloat16),
        scratch_shapes=[
            pltpu.VMEM((rows, length + 2 * LANES), jnp.float32),
            pltpu.VMEM((lanes, 2 * INNER), jnp.bfloat16),
            pltpu.VMEM((lanes, 2 * INNER), jnp.bfloat16),
        ],
        compiler_params=pltpu.CompilerParams(vmem_limit_bytes=48 * 2**20),
    )(blocks, jnp.asarray(taper_host(length)[None, :]), jnp.asarray(twiddle), jnp.asarray(high_table), jnp.asarray(low_table))


def row_kernel(shape, arrived, weight, twiddle, high_table, low_table, out, blocks, spread, folded):
    length, fold, step, parts, packed, factor = shape
    devices, tall, wide = arrived.shape
    per_device = packed // 2
    pieces = tall // packed
    code = arrived[...].astype(jnp.float32)
    scale = code[:, tall - packed :, wide - 1 :]
    value = decode(code, jnp.concatenate([scale] * pieces, axis=1))
    for piece in range(pieces):
        blocks[:, :, piece * wide : (piece + 1) * wide] = value[:, piece * packed : (piece + 1) * packed]
    width = blocks.shape[2]
    slots = LANES // step
    lane = lax.broadcasted_iota(jnp.int32, (packed, LANES), 1) // step
    sign = jnp.where(lax.broadcasted_iota(jnp.int32, (packed, INNER), 0) < per_device, 1.0, -1.0)

    for column in range(width // LANES):
        for half in range(devices // slots):
            tiles = [
                blocks[half * slots + g, :, column * LANES : (column + 1) * LANES] for g in range(slots)
            ]
            bit = 1
            while bit < slots:
                upper = (lane & bit) != 0
                for g in range(slots):
                    if g & bit:
                        continue
                    a, b = tiles[g], tiles[g + bit]
                    tiles[g] = jnp.where(upper, pltpu.roll(b, bit * step, 1), a)
                    tiles[g + bit] = jnp.where(upper, b, pltpu.roll(a, LANES - bit * step, 1))
                bit *= 2
            for g in range(slots):
                q = column * slots + g
                if q < fold * parts:
                    spread[q, :, half * LANES : (half + 1) * LANES] = tiles[g]

    def quarter(value):
        return pltpu.roll(value, per_device, 0) * sign

    place = lax.broadcasted_iota(jnp.int32, (packed, INNER), 1)
    for freq in range(fold):
        halo = spread[freq * parts + fold]
        run = 4 * step
        extra = {}
        for owner, (target, shift) in enumerate(
            ((fold - 2, -1), (fold - 1, -1 - step), (0, 2 * step), (1, step))
        ):
            inside = place != owner * step if owner < 2 else place != INNER - run + owner * step
            only = jnp.where((place % run == owner * step) & inside, halo, 0.0)
            moved = pltpu.roll(only, shift % INNER, 1)
            extra[target] = extra[target] + moved if target in extra else moved
        for point in range(fold):
            value = spread[freq * parts + point]
            if point in extra:
                value = value + extra[point]
            folded[(point * fold + freq) * packed : (point * fold + freq + 1) * packed, :] = (
                value * weight[point : point + 1, :]
            )

    high, low = split(folded[...])
    result = dot(high, high_table[...]) + dot(low, high_table[...]) + dot(high, low_table[...])
    for freq in range(fold):
        points = []
        for point in range(fold):
            begin = (point * fold + freq) * packed
            rows = slice(begin, begin + packed)
            value = result[rows, :INNER] + quarter(result[rows, INNER:])
            if point:
                tc = twiddle[point : point + 1, :INNER]
                ts = twiddle[point : point + 1, INNER:]
                value = value * tc + quarter(value) * ts
            points.append(value)
        half = fold // 2
        sums = [points[j] + points[fold - j] for j in range(1, half + 1)]
        differences = [quarter(points[j] - points[fold - j]) for j in range(1, half + 1)]

        def keep(index, value):
            power = value * value
            power = (power + pltpu.roll(power, per_device, 0)) * factor
            for side in range(INNER // LANES):
                row = (freq * length + index * INNER) // LANES + side
                rows = pl.ds(row, per_device, stride=fold * length // LANES)
                out[rows, :] = power[:per_device, side * LANES : (side + 1) * LANES]

        keep(0, functools.reduce(jnp.add, sums, points[0]))
        for index in range(1, half + 1):
            even, odd = points[0], None
            for j in range(1, half + 1):
                angle = 2 * math.pi * ((j * index) % fold) / fold
                even = even + math.cos(angle) * sums[j - 1]
                term = math.sin(angle) * differences[j - 1]
                odd = term if odd is None else odd + term
            keep(index, even + odd)
            keep(fold - index, even - odd)


def row_transform(arrived, length, rows):
    devices, tall, wide = arrived.shape
    packed = INNER // devices
    fold = length // INNER
    step = length // fold // devices
    angle = angles_host(np.arange(fold), np.arange(INNER), length)
    twiddle = np.concatenate([np.cos(angle), np.sin(angle)], axis=1).astype(np.float32)
    angle = angles_host(np.arange(INNER), np.arange(INNER), INNER)
    high_table, low_table = split_host(np.concatenate([np.cos(angle), np.sin(angle)], axis=1))
    parts = rows // step
    weight = np.ascontiguousarray(taper_host(length).reshape(INNER, fold).T)
    shape = (length, fold, step, parts, packed, STRIDE / (length * length))
    return pl.pallas_call(
        functools.partial(row_kernel, shape),
        out_shape=jax.ShapeDtypeStruct((fold * packed // 2 * length // LANES, LANES), jnp.float32),
        scratch_shapes=[
            pltpu.VMEM((devices, packed, tall * wide // packed), jnp.float32),
            pltpu.VMEM((fold * parts, packed, INNER), jnp.float32),
            pltpu.VMEM((fold * fold * packed, INNER), jnp.float32),
        ],
        compiler_params=pltpu.CompilerParams(vmem_limit_bytes=48 * 2**20),
    )(arrived, jnp.asarray(weight), jnp.asarray(twiddle), jnp.asarray(high_table), jnp.asarray(low_table))


def local(field):
    owners = lax.axis_size("cols")
    devices = lax.axis_size("rows") * owners
    length = field.shape[1] // STRIDE * lax.axis_size("rows")
    fold = length // INNER
    cut = cut_filter(field, owners, fold)
    grouped = lax.all_to_all(cut, "cols", split_axis=0, concat_axis=0, tiled=True)
    partial = column_transform(grouped, length, devices)
    arrived = lax.all_to_all(partial, ("rows", "cols"), split_axis=0, concat_axis=0, tiled=True)
    return row_transform(arrived, length, grouped.shape[1]).reshape(1, -1, length)


def solution(mesh):
    return jax.shard_map(
        local,
        mesh=mesh,
        in_specs=(P(None, "rows", "cols"),),
        out_specs=P(None, ("rows", "cols"), None),
        check_vma=False,
    )
```

time: 66.6 us -> 46.9 us (0.70)
  blocking collectives: 41.4 us -> 29.6 us
  Pallas kernels: 21.3 us -> 17.1 us
  local copies, waits for them, and re-layouts: 2.95 us -> 0.03 us
    all_to_all x1, blocking collectives: 25.3 us -> 17.9 us  [local(): lax.all_to_all(partial, ('rows', 'cols'), split_axis=0, concat_axis=0, ti...]
    pallas_call x1, Pallas kernels: 18.2 us -> 12.2 us  [cut_filter(): pl.pallas_call(functools.partial(cut_kernel, shape), out_shape=jax.ShapeD...]
    all_to_all x1, blocking collectives: 16 us -> 11.7 us  [local(): lax.all_to_all(cut, 'cols', split_axis=0, concat_axis=0, tiled=True)]
    unnamed x14, local copies, waits for them, and re-layouts: 1.88 us -> 0.03 us
    pallas_call x1 -> x0, local copies, waits for them, and re-layouts: 1.07 us -> none  [row_transform(): pl.pallas_call(functools.partial(row_kernel, shape), out_shape=jax.ShapeD...]
    pallas_call x1, Pallas kernels: 1.2 us -> 2.13 us  [column_transform(): pl.pallas_call(functools.partial(column_kernel, (owners, rows, own_cols,...]
    pallas_call x1, Pallas kernels: 1.88 us -> 2.77 us  [row_transform(): pl.pallas_call(functools.partial(row_kernel, shape), out_shape=jax.ShapeD...]
where the time goes in v1:
time: 46.9 us; the launch traced here: 46.7 us
  blocking collectives  29.6 us (63%)
  Pallas kernels  17.1 us (36%)
    all_to_all x1, blocking collectives, local(): lax.all_to_all(partial, ('rows', 'cols'), split_axis=0, concat_axis=0, ti...  17.9 us
    pallas_call x1, Pallas kernels, cut_filter(): pl.pallas_call(functools.partial(cut_kernel, shape), out_shape=jax.ShapeD...  12.2 us
    all_to_all x1, blocking collectives, local(): lax.all_to_all(cut, 'cols', split_axis=0, concat_axis=0, tiled=True)  11.7 us
    pallas_call x1, Pallas kernels, row_transform(): pl.pallas_call(functools.partial(row_kernel, shape), out_shape=jax.ShapeD...  2.77 us
    pallas_call x1, Pallas kernels, column_transform(): pl.pallas_call(functools.partial(column_kernel, (owners, rows, own_cols,...  2.13 us

profile of v1, /device:TPU:0, one launch (start us, length us, event | category | flops | bytes accessed | tf_op | source)
XLA Modules:
  0.0 46.7 jit_solution(12214761694070398119)
XLA Ops:
  0.0 0.0 copy-start.4
  0.0 0.0 copy-start.2
  0.0 0.0 copy-start.3
  0.0 0.0 copy-start.6
  0.0 0.0 copy-start
  0.0 0.0 copy-start.1
  0.0 0.0 copy-start.5
  0.0 12.2 %shard_map.91 = bf16[4,80,640]{2,1,0:T(8,128)(2,1)S(1)} custom-call(bf16[1,2304,4608]{2,1,0:T(8,128)(2,1)} %field.1), custom_call_target="tpu_custom_call" | custom-call | tf_op jit(solution)/shard_map/pallas_call | solution.py:177
  12.2 11.7 %all_to_all.10.blocks = bf16[4,80,640]{2,1,0:T(8,128)(2,1)S(1)} all-to-all(bf16[4,80,640]{2,1,0:T(8,128)(2,1)S(1)} %shard_map.91), channel_id=1, replica_groups=mesh['rows'=8,'cols'=4] {'cols'}, dimensions={0} | all-to-all | bytes 819200 | tf_op jit(solution)/shard_map/all_to_all | solution.py:413
  23.9 0.0 copy-done.4
  23.9 0.0 copy-done.2
  23.9 0.0 copy-done.3
  23.9 0.0 copy-done.6
  23.9 2.1 %shard_map.92 = bf16[32,16,384]{2,1,0:T(8,128)(2,1)S(1)} custom-call(bf16[4,80,640]{2,1,0:T(8,128)(2,1)S(1)} %all_to_all.10.blocks, f32[1,2304]{1,0:T(1,128)S(1)} %copy-done.6, f32[9,512]{1,0:T(8,128)S(1)} %copy-done.4, bf16[256,512]{1,0:T(8,128)(2,1)S(1)} %copy-done.3, bf16[256,512]{1,0:T(8,128)(2,1)S(1)} %copy-done.2), custom_call_target="tpu_custom_call" | custom-call | tf_op jit(solution)/shard_map/pallas_call | solution.py:276
  26.1 17.9 %all_to_all.11.arrived = bf16[32,16,384]{2,1,0:T(8,128)(2,1)S(1)} all-to-all(bf16[32,16,384]{2,1,0:T(8,128)(2,1)S(1)} %shard_map.92), channel_id=1, replica_groups=mesh['rows'=8,'cols'=4] {'rows','cols'}, dimensions={0} | all-to-all | bytes 786432 | tf_op jit(solution)/shard_map/all_to_all | solution.py:415
  43.9 0.0 copy-done
  43.9 0.0 copy-done.1
  43.9 0.0 copy-done.5
  44.0 2.8 %shard_map.93 = f32[648,128]{1,0:T(8,128)} custom-call(bf16[32,16,384]{2,1,0:T(8,128)(2,1)S(1)} %all_to_all.11.arrived, f32[9,256]{1,0:T(8,128)S(1)} %copy-done.5, f32[9,512]{1,0:T(8,128)S(1)} %copy-done.4, bf16[256,512]{1,0:T(8,128)(2,1)S(1)} %copy-done.1, bf16[256,512]{1,0:T(8,128)(2,1)S(1)} %copy-done), custom_call_target="tpu_custom_call" | custom-call | tf_op jit(solution)/shard_map/pallas_call | solution.py:395
Async XLA Ops:
  0.0 23.9 %copy-start.4 = (f32[9,512]{1,0:T(8,128)S(1)}, f32[9,512]{1,0:T(8,128)}, u32[]{:S(2)}) copy-start(f32[9,512]{1,0:T(8,128)} %constant.15.clone.twiddle) | copy-start | bytes 55300
  0.0 23.9 %copy-start.2 = (bf16[256,512]{1,0:T(8,128)(2,1)S(1)}, bf16[256,512]{1,0:T(8,128)(2,1)}, u32[]{:S(2)}) copy-start(bf16[256,512]{1,0:T(8,128)(2,1)} %constant.17.clone.low_table) | copy-start | bytes 786436
  0.0 23.9 %copy-start.3 = (bf16[256,512]{1,0:T(8,128)(2,1)S(1)}, bf16[256,512]{1,0:T(8,128)(2,1)}, u32[]{:S(2)}) copy-start(bf16[256,512]{1,0:T(8,128)(2,1)} %constant.16.clone.high_table) | copy-start | bytes 786436
  0.0 23.9 %copy-start.6 = (f32[1,2304]{1,0:T(1,128)S(1)}, f32[1,2304]{1,0:T(1,128)}, u32[]{:S(2)}) copy-start(f32[1,2304]{1,0:T(1,128)} %constant.14.clone.weight) | copy-start | bytes 27652
  0.0 43.9 %copy-start = (bf16[256,512]{1,0:T(8,128)(2,1)S(1)}, bf16[256,512]{1,0:T(8,128)(2,1)}, u32[]{:S(2)}) copy-start(bf16[256,512]{1,0:T(8,128)(2,1)} %constant.20.clone.low_table) | copy-start | bytes 786436
  0.0 43.9 %copy-start.1 = (bf16[256,512]{1,0:T(8,128)(2,1)S(1)}, bf16[256,512]{1,0:T(8,128)(2,1)}, u32[]{:S(2)}) copy-start(bf16[256,512]{1,0:T(8,128)(2,1)} %constant.19.clone.high_table) | copy-start | bytes 786436
  0.0 43.9 %copy-start.5 = (f32[9,256]{1,0:T(8,128)S(1)}, f32[9,256]{1,0:T(8,128)}, u32[]{:S(2)}) copy-start(f32[9,256]{1,0:T(8,128)} %constant.18.clone.weight) | copy-start | bytes 27652

commit v2 on v1

--- a/solution.py
+++ b/solution.py
@@ -91,7 +91,9 @@
     return lax.dot_general(left, right, (((1,), (1,)), ((), ())), preferred_element_type=jnp.float32)
 
 
-def cut_kernel(shape, field, out, raw, arrived, band_rows, band_cols, total, cut, ordered):
+def cut_kernel(shape, field, *refs):
+    outs, refs = refs[: shape[-2]], refs[shape[-2] :]
+    raw, arrived, band_rows, band_cols, sums_a, sums_b, total, cut, ordered = refs
     taps, chunks, groups, block_outs, fold, owners, own_rows = shape
     block_rows = raw.shape[1]
 
@@ -113,52 +115,74 @@
         both = [pltpu.roll(initial, move, 1) if move else initial for move in (2 * pair, 2 * pair + 1)]
         band_cols[16 * pair : 16 * pair + 16, :] = jnp.concatenate(both, axis=0).astype(jnp.bfloat16)
 
-    def step(chunk, carry):
+    places = cut.shape[0]
+    last = lax.broadcasted_iota(jnp.int32, (1, LANES), 1) == LANES - 1
+
+    def filter_cols(chunk, sums):
         copy(chunk).wait()
         stacked = jnp.concatenate(
             [raw[chunk, :, group * GROUP_COLS : (group + 1) * GROUP_COLS] for group in range(groups)], axis=0
         )
-        high, low = split(dot(stacked, band_cols[...]))
-        rows = pl.ds(pl.multiple_of(chunk * block_outs, 8), band_rows.shape[0])
+        sums[...] = dot(stacked, band_cols[...])
+
+    def finish(begin, count):
+        rows = pl.ds(begin, count)
+        middle = jnp.concatenate([total[1, rows, :], jnp.zeros((count, LANES), jnp.float32)], axis=1)
+        middle = pltpu.roll(middle, 64, 1)
+        joined = [
+            total[0, rows, :LANES],
+            total[0, rows, LANES:] + middle[:, :LANES],
+            middle[:, LANES : 2 * LANES],
+            middle[:, 2 * LANES :] + total[2, rows, :LANES],
+            total[2, rows, LANES:],
+        ]
+        scale = row_scale(*joined)
+        for place in range(places):
+            code = encode(joined[place], scale)
+            cut[place, rows, :] = jnp.where(last, scale, code) if place == places - 1 else code
+
+    def filter_rows(chunk, sums):
+        begin = pl.multiple_of(chunk * block_outs, 8)
+        high, low = split(sums[...])
+        rows = pl.ds(begin, band_rows.shape[0])
         for group in range(groups):
             own = slice(group * block_rows, (group + 1) * block_rows)
             term = dot(band_rows[...], high[own]) + dot(band_rows[...], low[own])
             total[group, rows, :] += term
+
+    filter_cols(0, sums_a)
+
+    def two(index, carry):
+        filter_cols(2 * index + 1, sums_b)
+        filter_rows(2 * index, sums_a)
+        filter_cols(2 * index + 2, sums_a)
+        filter_rows(2 * index + 1, sums_b)
         return carry
 
-    lax.fori_loop(0, chunks, step, 0)
-    count_rows = owners * own_rows + 2 * ROW_MARGIN
-    middle = jnp.concatenate([total[1], jnp.zeros((count_rows, LANES), jnp.float32)], axis=1)
-    middle = pltpu.roll(middle, 64, 1)
-    cut[0] = total[0, :, :LANES]
-    cut[1] = total[0, :, LANES:] + middle[:, :LANES]
-    cut[2] = middle[:, LANES : 2 * LANES]
-    cut[3] = middle[:, 2 * LANES :] + total[2, :, :LANES]
-    cut[4] = total[2, :, LANES:]
-    places = cut.shape[0]
-    scale = row_scale(*[cut[place] for place in range(places)])
-    last = lax.broadcasted_iota(jnp.int32, (count_rows, LANES), 1) == LANES - 1
-    for place in range(places):
-        code = encode(cut[place], scale)
-        cut[place] = jnp.where(last, scale, code) if place == places - 1 else code
+    lax.fori_loop(0, (chunks - 1) // 2, two, 0)
+    if chunks % 2 == 0:
+        filter_cols(chunks - 1, sums_b)
+        filter_rows(chunks - 2, sums_a)
+    filter_rows(chunks - 1, sums_a if chunks % 2 else sums_b)
+    finish(0, owners * own_rows + 2 * ROW_MARGIN)
     used = own_rows + 8
     sub = lax.broadcasted_iota(jnp.int32, (8, LANES), 0)
-    behind = ROW_MARGIN + owners * own_rows
     if ordered.shape[0] > used:
         ordered[used:, :] = jnp.full((ordered.shape[0] - used, ordered.shape[1]), NONE_CODE, jnp.float32)
-    for owner in range(owners):
+    own_col = lax.axis_index("cols")
+    for distance in range(owners):
+        owner = own_col ^ distance
+        count = own_rows // fold
         begin_at = ROW_MARGIN + owner * own_rows
-        count = own_rows // fold
-        edge = (ROW_MARGIN - 2, ROW_MARGIN - 1, 0, 1)[owner]
-        first = 0 if owner < 2 else behind
+        edge = jnp.where(owner < 2, ROW_MARGIN - 2 + owner, ROW_MARGIN + owners * own_rows + owner - 2)
         for place in range(places):
             lanes = slice(place * LANES, (place + 1) * LANES)
             for part in range(fold):
                 picked = cut[pl.ds(place, 1), pl.ds(begin_at + part, count, stride=fold), :]
                 ordered[part * count : (part + 1) * count, lanes] = picked[0]
-            block = pltpu.roll(cut[place, first : first + 8, :], (8 - edge) % 8, 0)
-            ordered[own_rows:used, lanes] = jnp.where(sub == 0, block, NONE_CODE)
-        out[owner] = ordered[...].astype(jnp.bfloat16)
+            row = cut[pl.ds(place, 1), pl.ds(edge, 1), :][0]
+            ordered[own_rows:used, lanes] = jnp.where(sub == 0, row, NONE_CODE)
+        outs[distance][...] = ordered[...].astype(jnp.bfloat16)
 
 
 def cut_filter(field, owners, fold):
@@ -176,14 +200,16 @@
     out_rows = ceil_to(own_rows + 8, 16)
     return pl.pallas_call(
         functools.partial(cut_kernel, shape),
-        out_shape=jax.ShapeDtypeStruct((owners, out_rows, out_cols), jnp.bfloat16),
+        out_shape=[jax.ShapeDtypeStruct((out_rows, out_cols), jnp.bfloat16)] * owners,
         in_specs=[pl.BlockSpec(memory_space=pl.ANY)],
-        out_specs=pl.BlockSpec(memory_space=pltpu.VMEM),
+        out_specs=[pl.BlockSpec(memory_space=pltpu.VMEM)] * owners,
         scratch_shapes=[
             pltpu.VMEM((chunks, block_rows, raw_cols), jnp.bfloat16),
             pltpu.SemaphoreType.DMA((chunks,)),
             pltpu.VMEM((span, block_rows), jnp.bfloat16),
             pltpu.VMEM((GROUP_COLS, 2 * LANES), jnp.bfloat16),
+            pltpu.VMEM((groups * block_rows, 2 * LANES), jnp.float32),
+            pltpu.VMEM((groups * block_rows, 2 * LANES), jnp.float32),
             pltpu.VMEM((groups, count_rows, 2 * LANES), jnp.float32),
             pltpu.VMEM((out_cols // LANES, count_rows, LANES), jnp.float32),
             pltpu.VMEM((out_rows, out_cols), jnp.float32),
@@ -192,19 +218,22 @@
     )(field)
 
 
-def column_kernel(shape, blocks, weight, twiddle, high_table, low_table, out, joined, high_rows, low_rows):
+def column_kernel(shape, *refs):
     owners, rows, own_cols, fold = shape
+    blocks, refs = refs[:owners], refs[owners:]
+    weight, twiddle, high_table, low_table, out, joined, high_rows, low_rows = refs
+    own_col = lax.axis_index("cols")
     joined[...] = jnp.zeros_like(joined)
-    width = blocks.shape[2]
+    width = blocks[0].shape[1]
     inside = lax.broadcasted_iota(jnp.int32, (rows, width), 1) < own_cols + 2 * HALO_OUTS
-    for owner in range(owners):
-        first = LANES + own_cols * owner - HALO_OUTS
-        code = blocks[owner].astype(jnp.float32)
+    for distance in range(owners):
+        first = LANES + own_cols * (own_col ^ distance) - HALO_OUTS
+        code = blocks[distance][...].astype(jnp.float32)
         value = decode(code, code[:, width - 1 :])
         value = jnp.where(inside, value, 0.0)
         block = jnp.concatenate([value, jnp.zeros((rows, LANES), jnp.float32)], axis=1)
-        base = first // LANES * LANES
-        joined[:, base : base + width + LANES] += pltpu.roll(block, first - base, 1)
+        base = pl.multiple_of(first // LANES * LANES, LANES)
+        joined[:, pl.ds(base, width + LANES)] += pltpu.roll(block, first % LANES, 1)
     points = [
         joined[:, LANES + INNER * i : LANES + INNER * (i + 1)] * weight[:, INNER * i : INNER * (i + 1)]
         for i in range(fold)
@@ -255,7 +284,8 @@
 
 
 def column_transform(blocks, length, devices):
-    owners, rows, width = blocks.shape
+    owners = len(blocks)
+    rows, width = blocks[0].shape
     own_cols = length // owners
     fold = length // INNER
     kept = INNER // 2
@@ -282,7 +312,7 @@
             pltpu.VMEM((lanes, 2 * INNER), jnp.bfloat16),
         ],
         compiler_params=pltpu.CompilerParams(vmem_limit_bytes=48 * 2**20),
-    )(blocks, jnp.asarray(taper_host(length)[None, :]), jnp.asarray(twiddle), jnp.asarray(high_table), jnp.asarray(low_table))
+    )(*blocks, jnp.asarray(taper_host(length)[None, :]), jnp.asarray(twiddle), jnp.asarray(high_table), jnp.asarray(low_table))
 
 
 def row_kernel(shape, arrived, weight, twiddle, high_table, low_table, out, blocks, spread, folded):
@@ -410,10 +440,13 @@
     length = field.shape[1] // STRIDE * lax.axis_size("rows")
     fold = length // INNER
     cut = cut_filter(field, owners, fold)
-    grouped = lax.all_to_all(cut, "cols", split_axis=0, concat_axis=0, tiled=True)
+    grouped = [cut[0]]
+    for distance in range(1, owners):
+        pairs = [(col, col ^ distance) for col in range(owners)]
+        grouped.append(lax.ppermute(cut[distance], "cols", pairs))
     partial = column_transform(grouped, length, devices)
     arrived = lax.all_to_all(partial, ("rows", "cols"), split_axis=0, concat_axis=0, tiled=True)
-    return row_transform(arrived, length, grouped.shape[1]).reshape(1, -1, length)
+    return row_transform(arrived, length, grouped[0].shape[0]).reshape(1, -1, length)
 
 
 def solution(mesh):

time: 46.9 us -> 47.4 us (1.011)
  blocking collectives: 29.6 us -> 18.9 us
  waiting for transfers between devices: 0 us -> 5.34 us
  starting transfers between devices: 0 us -> 3.2 us
  Pallas kernels: 17.1 us -> 19.8 us
    all_to_all x1 -> x0, blocking collectives: 11.7 us -> none  [local(): lax.all_to_all(cut, 'cols', split_axis=0, concat_axis=0, tiled=True)]
    ppermute x0 -> x3, waiting for transfers between devices: none -> 5.34 us  [local(): grouped.append(lax.ppermute(cut[distance], 'cols', pairs))]
    ppermute x0 -> x3, starting transfers between devices: none -> 3.2 us  [local(): grouped.append(lax.ppermute(cut[distance], 'cols', pairs))]
    pallas_call x1, Pallas kernels: 12.2 us -> 14.6 us  [cut_filter(): pl.pallas_call(functools.partial(cut_kernel, shape), out_shape=[jax.Shape...]
    all_to_all x1, blocking collectives: 17.9 us -> 18.9 us  [local(): lax.all_to_all(partial, ('rows', 'cols'), split_axis=0, concat_axis=0, ti...]
  transfers between devices with their start and end apart: 0 -> 3, of which waited for: 0 -> 2; matrix products, arithmetic and copies ran while one was open for 0% -> 0% of each run, Pallas kernels for 0% -> 0%
where the time goes in v2:
time: 47.4 us; the launch traced here: 47.3 us
  Pallas kernels  19.8 us (42%)
  blocking collectives  18.9 us (40%)
  waiting for transfers between devices  5.34 us (11%)
  starting transfers between devices  3.2 us (7%)
    all_to_all x1, blocking collectives, local(): lax.all_to_all(partial, ('rows', 'cols'), split_axis=0, concat_axis=0, ti...  18.9 us
    pallas_call x1, Pallas kernels, cut_filter(): pl.pallas_call(functools.partial(cut_kernel, shape), out_shape=[jax.Shape...  14.6 us
    ppermute x3, waiting for transfers between devices, local(): grouped.append(lax.ppermute(cut[distance], 'cols', pairs))  5.34 us
    ppermute x3, starting transfers between devices, local(): grouped.append(lax.ppermute(cut[distance], 'cols', pairs))  3.2 us
    pallas_call x1, Pallas kernels, row_transform(): pl.pallas_call(functools.partial(row_kernel, shape), out_shape=jax.ShapeD...  2.77 us
    pallas_call x1, Pallas kernels, column_transform(): pl.pallas_call(functools.partial(column_kernel, (owners, rows, own_cols,...  2.37 us
  transfers between devices with their start and end apart: 3, of which 2 were waited for; matrix products, arithmetic and copies ran while one was open for 0% of the time, Pallas kernels for 0%

profile of v2, /device:TPU:0, one launch (start us, length us, event | category | flops | bytes accessed | tf_op | source)
XLA Modules:
  0.0 47.3 jit_solution(2966225956981490468)
XLA Ops:
  0.0 0.0 copy-start.4
  0.0 0.0 copy-start.2
  0.0 0.0 copy-start.3
  0.0 0.0 copy-start.6
  0.0 0.0 copy-start
  0.0 0.0 copy-start.1
  0.0 0.0 copy-start.5
  0.0 14.6 %shard_map.91 = (bf16[80,640]{1,0:T(8,128)(2,1)S(1)}, bf16[80,640]{1,0:T(8,128)(2,1)S(1)}, bf16[80,640]{1,0:T(8,128)(2,1)S(1)}, bf16[80,640]{1,0:T(8,128)(2,1)S(1)}) custom-call(bf16[1,2304,4608]{2,1,0:T(8,128)(2,1)} %field.1), custom_call_target="tpu_custom_call" | custom-call | tf_op jit(solution)/shard_map/pallas_call | solution.py:201
  14.7 0.5 %collective-permute-start = (bf16[80,640]{1,0:T(8,128)(2,1)S(1)}, bf16[80,640]{1,0:T(8,128)(2,1)S(1)}, u32[]{:S(2)}, u32[]{:S(2)}) collective-permute-start(bf16[80,640]{1,0:T(8,128)(2,1)S(1)} %get-tuple-element.10), channel_id=1, source_target_pairs={{0,1},{1,0},{2,3},{3,2},{4,5},{5,4},{6,7},{7,6},{8,9},{9,8},{10,11... | collective-permute-start | bytes 307208 | tf_op jit(solution)/shard_map/ppermute | solution.py:446
  15.2 2.6 %collective-permute-start.1 = (bf16[80,640]{1,0:T(8,128)(2,1)S(1)}, bf16[80,640]{1,0:T(8,128)(2,1)S(1)}, u32[]{:S(2)}, u32[]{:S(2)}) collective-permute-start(bf16[80,640]{1,0:T(8,128)(2,1)S(1)} %get-tuple-element.11), channel_id=1, source_target_pairs={{0,2},{1,3},{2,0},{3,1},{4,6},{5,7},{6,4},{7,5},{8,10},{9,11},{10,... | collective-permute-start | bytes 307208 | tf_op jit(solution)/shard_map/ppermute | solution.py:446
  17.8 0.1 collective-permute-start.2
  17.9 0.0 collective-permute-done.refs_1_
  17.9 3.7 %collective-permute-done.1.refs_2_ = bf16[80,640]{1,0:T(8,128)(2,1)S(1)} collective-permute-done((bf16[80,640]{1,0:T(8,128)(2,1)S(1)}, bf16[80,640]{1,0:T(8,128)(2,1)S(1)}, u32[]{:S(2)}, u32[]{:S(2)}) %collective-permute-start.1) | collective-permute-done | bytes 102432 | tf_op jit(solution)/shard_map/ppermute | solution.py:446
  21.5 1.7 %collective-permute-done.2.refs_3_ = bf16[80,640]{1,0:T(8,128)(2,1)S(1)} collective-permute-done((bf16[80,640]{1,0:T(8,128)(2,1)S(1)}, bf16[80,640]{1,0:T(8,128)(2,1)S(1)}, u32[]{:S(2)}, u32[]{:S(2)}) %collective-permute-start.2) | collective-permute-done | bytes 102432 | tf_op jit(solution)/shard_map/ppermute | solution.py:446
  23.2 0.0 copy-done.4
  23.2 0.0 copy-done.2
  23.2 0.0 copy-done.3
  23.2 0.0 copy-done.6
  23.2 2.4 %shard_map.92 = bf16[32,16,384]{2,1,0:T(8,128)(2,1)S(1)} custom-call(bf16[80,640]{1,0:T(8,128)(2,1)S(1)} %get-tuple-element.9.refs_0_, bf16[80,640]{1,0:T(8,128)(2,1)S(1)} %collective-permute-done.refs_1_, bf16[80,640]{1,0:T(8,128)(2,1)S(1)} %collective-permute-done.1.refs_2_, bf16[80,640]{1,0:T(8,128)(2,1)S(1)} %collective-permute-done.2.refs_3_, ...), custom_call_target="tpu_custom_call" | custom-call | tf_op jit(solution)/shard_map/pallas_call | solution.py:306
  25.6 18.9 %all_to_all.5.arrived = bf16[32,16,384]{2,1,0:T(8,128)(2,1)S(1)} all-to-all(bf16[32,16,384]{2,1,0:T(8,128)(2,1)S(1)} %shard_map.92), channel_id=1, replica_groups=mesh['rows'=8,'cols'=4] {'rows','cols'}, dimensions={0} | all-to-all | bytes 786432 | tf_op jit(solution)/shard_map/all_to_all | solution.py:448
  44.5 0.0 copy-done
  44.5 0.0 copy-done.1
  44.5 0.0 copy-done.5
  44.5 2.8 %shard_map.93 = f32[648,128]{1,0:T(8,128)} custom-call(bf16[32,16,384]{2,1,0:T(8,128)(2,1)S(1)} %all_to_all.5.arrived, f32[9,256]{1,0:T(8,128)S(1)} %copy-done.5, f32[9,512]{1,0:T(8,128)S(1)} %copy-done.4, bf16[256,512]{1,0:T(8,128)(2,1)S(1)} %copy-done.1, bf16[256,512]{1,0:T(8,128)(2,1)S(1)} %copy-done), custom_call_target="tpu_custom_call" | custom-call | tf_op jit(solution)/shard_map/pallas_call | solution.py:425
Async XLA Ops:
  0.0 23.2 %copy-start.4 = (f32[9,512]{1,0:T(8,128)S(1)}, f32[9,512]{1,0:T(8,128)}, u32[]{:S(2)}) copy-start(f32[9,512]{1,0:T(8,128)} %constant.15.clone.refs_5_.twiddle) | copy-start | bytes 55300
  0.0 23.2 %copy-start.2 = (bf16[256,512]{1,0:T(8,128)(2,1)S(1)}, bf16[256,512]{1,0:T(8,128)(2,1)}, u32[]{:S(2)}) copy-start(bf16[256,512]{1,0:T(8,128)(2,1)} %constant.17.clone.refs_7_) | copy-start | bytes 786436
  0.0 23.2 %copy-start.3 = (bf16[256,512]{1,0:T(8,128)(2,1)S(1)}, bf16[256,512]{1,0:T(8,128)(2,1)}, u32[]{:S(2)}) copy-start(bf16[256,512]{1,0:T(8,128)(2,1)} %constant.16.clone.refs_6_) | copy-start | bytes 786436
  0.0 23.2 %copy-start.6 = (f32[1,2304]{1,0:T(1,128)S(1)}, f32[1,2304]{1,0:T(1,128)}, u32[]{:S(2)}) copy-start(f32[1,2304]{1,0:T(1,128)} %constant.14.clone.refs_4_) | copy-start | bytes 27652
  0.0 44.5 %copy-start = (bf16[256,512]{1,0:T(8,128)(2,1)S(1)}, bf16[256,512]{1,0:T(8,128)(2,1)}, u32[]{:S(2)}) copy-start(bf16[256,512]{1,0:T(8,128)(2,1)} %constant.20.clone.low_table) | copy-start | bytes 786436
  0.0 44.5 %copy-start.1 = (bf16[256,512]{1,0:T(8,128)(2,1)S(1)}, bf16[256,512]{1,0:T(8,128)(2,1)}, u32[]{:S(2)}) copy-start(bf16[256,512]{1,0:T(8,128)(2,1)} %constant.19.clone.high_table) | copy-start | bytes 786436
  0.0 44.5 %copy-start.5 = (f32[9,256]{1,0:T(8,128)S(1)}, f32[9,256]{1,0:T(8,128)}, u32[]{:S(2)}) copy-start(f32[9,256]{1,0:T(8,128)} %constant.18.clone.weight) | copy-start | bytes 27652
  14.7 3.2 %collective-permute-start = (bf16[80,640]{1,0:T(8,128)(2,1)S(1)}, bf16[80,640]{1,0:T(8,128)(2,1)S(1)}, u32[]{:S(2)}, u32[]{:S(2)}) collective-permute-start(bf16[80,640]{1,0:T(8,128)(2,1)S(1)} %get-tuple-element.10), channel_id=1, source_target_pairs={{0,1},{1,0},{2,3},{3,2},{4,5},{5,4},{6,7},{7,6},{8,9},{9,8},{10,11... | collective-permute-start | bytes 307208 | tf_op jit(solution)/shard_map/ppermute | solution.py:446
  15.2 6.3 %collective-permute-start.1 = (bf16[80,640]{1,0:T(8,128)(2,1)S(1)}, bf16[80,640]{1,0:T(8,128)(2,1)S(1)}, u32[]{:S(2)}, u32[]{:S(2)}) collective-permute-start(bf16[80,640]{1,0:T(8,128)(2,1)S(1)} %get-tuple-element.11), channel_id=1, source_target_pairs={{0,2},{1,3},{2,0},{3,1},{4,6},{5,7},{6,4},{7,5},{8,10},{9,11},{10,... | collective-permute-start | bytes 307208 | tf_op jit(solution)/shard_map/ppermute | solution.py:446
  17.8 5.4 %collective-permute-start.2 = (bf16[80,640]{1,0:T(8,128)(2,1)S(1)}, bf16[80,640]{1,0:T(8,128)(2,1)S(1)}, u32[]{:S(2)}, u32[]{:S(2)}) collective-permute-start(bf16[80,640]{1,0:T(8,128)(2,1)S(1)} %get-tuple-element.12), channel_id=1, source_target_pairs={{0,3},{1,2},{2,1},{3,0},{4,7},{5,6},{6,5},{7,4},{8,11},{9,10},{10,... | collective-permute-start | bytes 307208 | tf_op jit(solution)/shard_map/ppermute | solution.py:446

commit v3 on v2

--- a/solution.py
+++ b/solution.py
@@ -93,7 +93,7 @@
 
 def cut_kernel(shape, field, *refs):
     outs, refs = refs[: shape[-2]], refs[shape[-2] :]
-    raw, arrived, band_rows, band_cols, sums_a, sums_b, total, cut, ordered = refs
+    raw, arrived, band_rows, band_cols, sums_a, sums_b, total, cut, ordered, coded = refs
     taps, chunks, groups, block_outs, fold, owners, own_rows = shape
     block_rows = raw.shape[1]
 
@@ -149,6 +149,7 @@
             own = slice(group * block_rows, (group + 1) * block_rows)
             term = dot(band_rows[...], high[own]) + dot(band_rows[...], low[own])
             total[group, rows, :] += term
+        finish(begin, block_outs)
 
     filter_cols(0, sums_a)
 
@@ -164,25 +165,26 @@
         filter_cols(chunks - 1, sums_b)
         filter_rows(chunks - 2, sums_a)
     filter_rows(chunks - 1, sums_a if chunks % 2 else sums_b)
-    finish(0, owners * own_rows + 2 * ROW_MARGIN)
+    finish(owners * own_rows, 2 * ROW_MARGIN)
     used = own_rows + 8
     sub = lax.broadcasted_iota(jnp.int32, (8, LANES), 0)
     if ordered.shape[0] > used:
         ordered[used:, :] = jnp.full((ordered.shape[0] - used, ordered.shape[1]), NONE_CODE, jnp.float32)
-    own_col = lax.axis_index("cols")
-    for distance in range(owners):
-        owner = own_col ^ distance
+    for owner in range(owners):
         count = own_rows // fold
         begin_at = ROW_MARGIN + owner * own_rows
-        edge = jnp.where(owner < 2, ROW_MARGIN - 2 + owner, ROW_MARGIN + owners * own_rows + owner - 2)
+        edge = (ROW_MARGIN - 2, ROW_MARGIN - 1, ROW_MARGIN + owners * own_rows, ROW_MARGIN + owners * own_rows + 1)[owner]
         for place in range(places):
             lanes = slice(place * LANES, (place + 1) * LANES)
             for part in range(fold):
                 picked = cut[pl.ds(place, 1), pl.ds(begin_at + part, count, stride=fold), :]
                 ordered[part * count : (part + 1) * count, lanes] = picked[0]
-            row = cut[pl.ds(place, 1), pl.ds(edge, 1), :][0]
+            row = cut[place, edge : edge + 1, :]
             ordered[own_rows:used, lanes] = jnp.where(sub == 0, row, NONE_CODE)
-        outs[distance][...] = ordered[...].astype(jnp.bfloat16)
+        coded[owner] = ordered[...].astype(jnp.bfloat16)
+    own_col = lax.axis_index("cols")
+    for distance in range(owners):
+        outs[distance][...] = coded[own_col ^ distance]
 
 
 def cut_filter(field, owners, fold):
@@ -213,6 +215,7 @@
             pltpu.VMEM((groups, count_rows, 2 * LANES), jnp.float32),
             pltpu.VMEM((out_cols // LANES, count_rows, LANES), jnp.float32),
             pltpu.VMEM((out_rows, out_cols), jnp.float32),
+            pltpu.VMEM((owners, out_rows, out_cols), jnp.bfloat16),
         ],
         compiler_params=pltpu.CompilerParams(vmem_limit_bytes=40 * 2**20),
     )(field)

time: 47.4 us -> 47.2 us (level)
  no operation moved by 1% of the time
where the time goes in v3:
time: 47.2 us; the launch traced here: 47 us
  Pallas kernels  19.5 us (41%)
  blocking collectives  18.9 us (40%)
  waiting for transfers between devices  5.34 us (11%)
  starting transfers between devices  3.2 us (7%)
    all_to_all x1, blocking collectives, local(): lax.all_to_all(partial, ('rows', 'cols'), split_axis=0, concat_axis=0, ti...  18.9 us
    pallas_call x1, Pallas kernels, cut_filter(): pl.pallas_call(functools.partial(cut_kernel, shape), out_shape=[jax.Shape...  14.4 us
    ppermute x3, waiting for transfers between devices, local(): grouped.append(lax.ppermute(cut[distance], 'cols', pairs))  5.34 us
    ppermute x3, starting transfers between devices, local(): grouped.append(lax.ppermute(cut[distance], 'cols', pairs))  3.2 us
    pallas_call x1, Pallas kernels, row_transform(): pl.pallas_call(functools.partial(row_kernel, shape), out_shape=jax.ShapeD...  2.77 us
    pallas_call x1, Pallas kernels, column_transform(): pl.pallas_call(functools.partial(column_kernel, (owners, rows, own_cols,...  2.37 us
  transfers between devices with their start and end apart: 3, of which 2 were waited for; matrix products, arithmetic and copies ran while one was open for 0% of the time, Pallas kernels for 0%

profile of v3, /device:TPU:0, one launch (start us, length us, event | category | flops | bytes accessed | tf_op | source)
XLA Modules:
  0.0 47.0 jit_solution(1691328964463986807)
XLA Ops:
  0.0 0.0 copy-start.4
  0.0 0.0 copy-start.2
  0.0 0.0 copy-start.3
  0.0 0.0 copy-start.6
  0.0 0.0 copy-start
  0.0 0.0 copy-start.1
  0.0 0.0 copy-start.5
  0.0 14.4 %shard_map.91 = (bf16[80,640]{1,0:T(8,128)(2,1)S(1)}, bf16[80,640]{1,0:T(8,128)(2,1)S(1)}, bf16[80,640]{1,0:T(8,128)(2,1)S(1)}, bf16[80,640]{1,0:T(8,128)(2,1)S(1)}) custom-call(bf16[1,2304,4608]{2,1,0:T(8,128)(2,1)} %field.1), custom_call_target="tpu_custom_call" | custom-call | tf_op jit(solution)/shard_map/pallas_call | solution.py:203
  14.4 0.5 %collective-permute-start = (bf16[80,640]{1,0:T(8,128)(2,1)S(1)}, bf16[80,640]{1,0:T(8,128)(2,1)S(1)}, u32[]{:S(2)}, u32[]{:S(2)}) collective-permute-start(bf16[80,640]{1,0:T(8,128)(2,1)S(1)} %get-tuple-element.10), channel_id=1, source_target_pairs={{0,1},{1,0},{2,3},{3,2},{4,5},{5,4},{6,7},{7,6},{8,9},{9,8},{10,11... | collective-permute-start | bytes 307208 | tf_op jit(solution)/shard_map/ppermute | solution.py:449
  15.0 2.6 %collective-permute-start.1 = (bf16[80,640]{1,0:T(8,128)(2,1)S(1)}, bf16[80,640]{1,0:T(8,128)(2,1)S(1)}, u32[]{:S(2)}, u32[]{:S(2)}) collective-permute-start(bf16[80,640]{1,0:T(8,128)(2,1)S(1)} %get-tuple-element.11), channel_id=1, source_target_pairs={{0,2},{1,3},{2,0},{3,1},{4,6},{5,7},{6,4},{7,5},{8,10},{9,11},{10,... | collective-permute-start | bytes 307208 | tf_op jit(solution)/shard_map/ppermute | solution.py:449
  17.6 0.1 collective-permute-start.2
  17.6 0.0 collective-permute-done.refs_1_
  17.7 3.7 %collective-permute-done.1.refs_2_ = bf16[80,640]{1,0:T(8,128)(2,1)S(1)} collective-permute-done((bf16[80,640]{1,0:T(8,128)(2,1)S(1)}, bf16[80,640]{1,0:T(8,128)(2,1)S(1)}, u32[]{:S(2)}, u32[]{:S(2)}) %collective-permute-start.1) | collective-permute-done | bytes 102432 | tf_op jit(solution)/shard_map/ppermute | solution.py:449
  21.3 1.7 %collective-permute-done.2.refs_3_ = bf16[80,640]{1,0:T(8,128)(2,1)S(1)} collective-permute-done((bf16[80,640]{1,0:T(8,128)(2,1)S(1)}, bf16[80,640]{1,0:T(8,128)(2,1)S(1)}, u32[]{:S(2)}, u32[]{:S(2)}) %collective-permute-start.2) | collective-permute-done | bytes 102432 | tf_op jit(solution)/shard_map/ppermute | solution.py:449
  23.0 0.0 copy-done.4
  23.0 0.0 copy-done.2
  23.0 0.0 copy-done.3
  23.0 0.0 copy-done.6
  23.0 2.4 %shard_map.92 = bf16[32,16,384]{2,1,0:T(8,128)(2,1)S(1)} custom-call(bf16[80,640]{1,0:T(8,128)(2,1)S(1)} %get-tuple-element.9.refs_0_, bf16[80,640]{1,0:T(8,128)(2,1)S(1)} %collective-permute-done.refs_1_, bf16[80,640]{1,0:T(8,128)(2,1)S(1)} %collective-permute-done.1.refs_2_, bf16[80,640]{1,0:T(8,128)(2,1)S(1)} %collective-permute-done.2.refs_3_, ...), custom_call_target="tpu_custom_call" | custom-call | tf_op jit(solution)/shard_map/pallas_call | solution.py:309
  25.4 18.9 %all_to_all.5.arrived = bf16[32,16,384]{2,1,0:T(8,128)(2,1)S(1)} all-to-all(bf16[32,16,384]{2,1,0:T(8,128)(2,1)S(1)} %shard_map.92), channel_id=1, replica_groups=mesh['rows'=8,'cols'=4] {'rows','cols'}, dimensions={0} | all-to-all | bytes 786432 | tf_op jit(solution)/shard_map/all_to_all | solution.py:451
  44.3 0.0 copy-done
  44.3 0.0 copy-done.1
  44.3 0.0 copy-done.5
  44.3 2.8 %shard_map.93 = f32[648,128]{1,0:T(8,128)} custom-call(bf16[32,16,384]{2,1,0:T(8,128)(2,1)S(1)} %all_to_all.5.arrived, f32[9,256]{1,0:T(8,128)S(1)} %copy-done.5, f32[9,512]{1,0:T(8,128)S(1)} %copy-done.4, bf16[256,512]{1,0:T(8,128)(2,1)S(1)} %copy-done.1, bf16[256,512]{1,0:T(8,128)(2,1)S(1)} %copy-done), custom_call_target="tpu_custom_call" | custom-call | tf_op jit(solution)/shard_map/pallas_call | solution.py:428
Async XLA Ops:
  0.0 23.0 %copy-start.4 = (f32[9,512]{1,0:T(8,128)S(1)}, f32[9,512]{1,0:T(8,128)}, u32[]{:S(2)}) copy-start(f32[9,512]{1,0:T(8,128)} %constant.15.clone.refs_5_.twiddle) | copy-start | bytes 55300
  0.0 23.0 %copy-start.2 = (bf16[256,512]{1,0:T(8,128)(2,1)S(1)}, bf16[256,512]{1,0:T(8,128)(2,1)}, u32[]{:S(2)}) copy-start(bf16[256,512]{1,0:T(8,128)(2,1)} %constant.17.clone.refs_7_) | copy-start | bytes 786436
  0.0 23.0 %copy-start.3 = (bf16[256,512]{1,0:T(8,128)(2,1)S(1)}, bf16[256,512]{1,0:T(8,128)(2,1)}, u32[]{:S(2)}) copy-start(bf16[256,512]{1,0:T(8,128)(2,1)} %constant.16.clone.refs_6_) | copy-start | bytes 786436
  0.0 23.0 %copy-start.6 = (f32[1,2304]{1,0:T(1,128)S(1)}, f32[1,2304]{1,0:T(1,128)}, u32[]{:S(2)}) copy-start(f32[1,2304]{1,0:T(1,128)} %constant.14.clone.refs_4_) | copy-start | bytes 27652
  0.0 44.3 %copy-start = (bf16[256,512]{1,0:T(8,128)(2,1)S(1)}, bf16[256,512]{1,0:T(8,128)(2,1)}, u32[]{:S(2)}) copy-start(bf16[256,512]{1,0:T(8,128)(2,1)} %constant.20.clone.low_table) | copy-start | bytes 786436
  0.0 44.3 %copy-start.1 = (bf16[256,512]{1,0:T(8,128)(2,1)S(1)}, bf16[256,512]{1,0:T(8,128)(2,1)}, u32[]{:S(2)}) copy-start(bf16[256,512]{1,0:T(8,128)(2,1)} %constant.19.clone.high_table) | copy-start | bytes 786436
  0.0 44.2 %copy-start.5 = (f32[9,256]{1,0:T(8,128)S(1)}, f32[9,256]{1,0:T(8,128)}, u32[]{:S(2)}) copy-start(f32[9,256]{1,0:T(8,128)} %constant.18.clone.weight) | copy-start | bytes 27652
  14.4 3.2 %collective-permute-start = (bf16[80,640]{1,0:T(8,128)(2,1)S(1)}, bf16[80,640]{1,0:T(8,128)(2,1)S(1)}, u32[]{:S(2)}, u32[]{:S(2)}) collective-permute-start(bf16[80,640]{1,0:T(8,128)(2,1)S(1)} %get-tuple-element.10), channel_id=1, source_target_pairs={{0,1},{1,0},{2,3},{3,2},{4,5},{5,4},{6,7},{7,6},{8,9},{9,8},{10,11... | collective-permute-start | bytes 307208 | tf_op jit(solution)/shard_map/ppermute | solution.py:449
  15.0 6.3 %collective-permute-start.1 = (bf16[80,640]{1,0:T(8,128)(2,1)S(1)}, bf16[80,640]{1,0:T(8,128)(2,1)S(1)}, u32[]{:S(2)}, u32[]{:S(2)}) collective-permute-start(bf16[80,640]{1,0:T(8,128)(2,1)S(1)} %get-tuple-element.11), channel_id=1, source_target_pairs={{0,2},{1,3},{2,0},{3,1},{4,6},{5,7},{6,4},{7,5},{8,10},{9,11},{10,... | collective-permute-start | bytes 307208 | tf_op jit(solution)/shard_map/ppermute | solution.py:449
  17.6 5.4 %collective-permute-start.2 = (bf16[80,640]{1,0:T(8,128)(2,1)S(1)}, bf16[80,640]{1,0:T(8,128)(2,1)S(1)}, u32[]{:S(2)}, u32[]{:S(2)}) collective-permute-start(bf16[80,640]{1,0:T(8,128)(2,1)S(1)} %get-tuple-element.12), channel_id=1, source_target_pairs={{0,3},{1,2},{2,1},{3,0},{4,7},{5,6},{6,5},{7,4},{8,11},{9,10},{10,... | collective-permute-start | bytes 307208 | tf_op jit(solution)/shard_map/ppermute | solution.py:449

commit v4 on v3

--- a/solution.py
+++ b/solution.py
@@ -93,7 +93,7 @@
 
 def cut_kernel(shape, field, *refs):
     outs, refs = refs[: shape[-2]], refs[shape[-2] :]
-    raw, arrived, band_rows, band_cols, sums_a, sums_b, total, cut, ordered, coded = refs
+    raw, arrived, band_rows, band_cols, total, cut, ordered, coded = refs
     taps, chunks, groups, block_outs, fold, owners, own_rows = shape
     block_rows = raw.shape[1]
 
@@ -104,9 +104,11 @@
     for chunk in range(chunks):
         copy(chunk).start()
     total[...] = jnp.zeros_like(total)
-    ids = lax.broadcasted_iota(jnp.int32, band_rows.shape, 1)
-    ids = ids - STRIDE * (lax.broadcasted_iota(jnp.int32, band_rows.shape, 0) - ROW_MARGIN) + REACH
-    band_rows[...] = band(taps, ids).astype(jnp.bfloat16)
+    shape_rows = (band_rows.shape[0], block_rows)
+    ids = lax.broadcasted_iota(jnp.int32, shape_rows, 1)
+    ids = ids - STRIDE * (lax.broadcasted_iota(jnp.int32, shape_rows, 0) - ROW_MARGIN) + REACH
+    rows_band = band(taps, ids).astype(jnp.bfloat16)
+    band_rows[...] = jnp.concatenate([rows_band, rows_band], axis=1)
     shape_8 = (8, band_cols.shape[1])
     ids = lax.broadcasted_iota(jnp.int32, shape_8, 0)
     ids = ids - STRIDE * (lax.broadcasted_iota(jnp.int32, shape_8, 1) - HALO_OUTS) + REACH
@@ -117,13 +119,6 @@
 
     places = cut.shape[0]
     last = lax.broadcasted_iota(jnp.int32, (1, LANES), 1) == LANES - 1
-
-    def filter_cols(chunk, sums):
-        copy(chunk).wait()
-        stacked = jnp.concatenate(
-            [raw[chunk, :, group * GROUP_COLS : (group + 1) * GROUP_COLS] for group in range(groups)], axis=0
-        )
-        sums[...] = dot(stacked, band_cols[...])
 
     def finish(begin, count):
         rows = pl.ds(begin, count)
@@ -141,31 +136,17 @@
             code = encode(joined[place], scale)
             cut[place, rows, :] = jnp.where(last, scale, code) if place == places - 1 else code
 
-    def filter_rows(chunk, sums):
+    def step(chunk, carry):
+        copy(chunk).wait()
         begin = pl.multiple_of(chunk * block_outs, 8)
-        high, low = split(sums[...])
         rows = pl.ds(begin, band_rows.shape[0])
         for group in range(groups):
-            own = slice(group * block_rows, (group + 1) * block_rows)
-            term = dot(band_rows[...], high[own]) + dot(band_rows[...], low[own])
-            total[group, rows, :] += term
-        finish(begin, block_outs)
-
-    filter_cols(0, sums_a)
-
-    def two(index, carry):
-        filter_cols(2 * index + 1, sums_b)
-        filter_rows(2 * index, sums_a)
-        filter_cols(2 * index + 2, sums_a)
-        filter_rows(2 * index + 1, sums_b)
+            high, low = split(dot(raw[chunk, :, group * GROUP_COLS : (group + 1) * GROUP_COLS], band_cols[...]))
+            total[group, rows, :] += dot(band_rows[...], jnp.concatenate([high, low], axis=0))
         return carry
 
-    lax.fori_loop(0, (chunks - 1) // 2, two, 0)
-    if chunks % 2 == 0:
-        filter_cols(chunks - 1, sums_b)
-        filter_rows(chunks - 2, sums_a)
-    filter_rows(chunks - 1, sums_a if chunks % 2 else sums_b)
-    finish(owners * own_rows, 2 * ROW_MARGIN)
+    lax.fori_loop(0, chunks, step, 0)
+    finish(0, owners * own_rows + 2 * ROW_MARGIN)
     used = own_rows + 8
     sub = lax.broadcasted_iota(jnp.int32, (8, LANES), 0)
     if ordered.shape[0] > used:
@@ -208,10 +189,8 @@
         scratch_shapes=[
             pltpu.VMEM((chunks, block_rows, raw_cols), jnp.bfloat16),
             pltpu.SemaphoreType.DMA((chunks,)),
-            pltpu.VMEM((span, block_rows), jnp.bfloat16),
+            pltpu.VMEM((span, 2 * block_rows), jnp.bfloat16),
             pltpu.VMEM((GROUP_COLS, 2 * LANES), jnp.bfloat16),
-            pltpu.VMEM((groups * block_rows, 2 * LANES), jnp.float32),
-            pltpu.VMEM((groups * block_rows, 2 * LANES), jnp.float32),
             pltpu.VMEM((groups, count_rows, 2 * LANES), jnp.float32),
             pltpu.VMEM((out_cols // LANES, count_rows, LANES), jnp.float32),
             pltpu.VMEM((out_rows, out_cols), jnp.float32),

time: 47.2 us -> 51.5 us (1.091)
  Pallas kernels: 19.5 us -> 23.8 us
    pallas_call x1, Pallas kernels: 14.4 us -> 18.7 us  [cut_filter(): pl.pallas_call(functools.partial(cut_kernel, shape), out_shape=[jax.Shape...]
where the time goes in v4:
time: 51.5 us; the launch traced here: 51.3 us
  Pallas kernels  23.8 us (46%)
  blocking collectives  18.9 us (37%)
  waiting for transfers between devices  5.34 us (10%)
  starting transfers between devices  3.21 us (6%)
    all_to_all x1, blocking collectives, local(): lax.all_to_all(partial, ('rows', 'cols'), split_axis=0, concat_axis=0, ti...  18.9 us
    pallas_call x1, Pallas kernels, cut_filter(): pl.pallas_call(functools.partial(cut_kernel, shape), out_shape=[jax.Shape...  18.7 us
    ppermute x3, waiting for transfers between devices, local(): grouped.append(lax.ppermute(cut[distance], 'cols', pairs))  5.34 us
    ppermute x3, starting transfers between devices, local(): grouped.append(lax.ppermute(cut[distance], 'cols', pairs))  3.21 us
    pallas_call x1, Pallas kernels, row_transform(): pl.pallas_call(functools.partial(row_kernel, shape), out_shape=jax.ShapeD...  2.77 us
    pallas_call x1, Pallas kernels, column_transform(): pl.pallas_call(functools.partial(column_kernel, (owners, rows, own_cols,...  2.37 us
  transfers between devices with their start and end apart: 3, of which 2 were waited for; matrix products, arithmetic and copies ran while one was open for 0% of the time, Pallas kernels for 0%

profile of v4, /device:TPU:0, one launch (start us, length us, event | category | flops | bytes accessed | tf_op | source)
XLA Modules:
  0.0 51.3 jit_solution(14155179862257836593)
XLA Ops:
  0.0 0.0 copy-start.4
  0.0 0.0 copy-start.2
  0.0 0.0 copy-start.3
  0.0 0.0 copy-start.6
  0.0 0.0 copy-start
  0.0 0.0 copy-start.1
  0.0 0.0 copy-start.5
  0.0 18.7 %shard_map.91 = (bf16[80,640]{1,0:T(8,128)(2,1)S(1)}, bf16[80,640]{1,0:T(8,128)(2,1)S(1)}, bf16[80,640]{1,0:T(8,128)(2,1)S(1)}, bf16[80,640]{1,0:T(8,128)(2,1)S(1)}) custom-call(bf16[1,2304,4608]{2,1,0:T(8,128)(2,1)} %field.1), custom_call_target="tpu_custom_call" | custom-call | tf_op jit(solution)/shard_map/pallas_call | solution.py:184
  18.7 0.5 %collective-permute-start = (bf16[80,640]{1,0:T(8,128)(2,1)S(1)}, bf16[80,640]{1,0:T(8,128)(2,1)S(1)}, u32[]{:S(2)}, u32[]{:S(2)}) collective-permute-start(bf16[80,640]{1,0:T(8,128)(2,1)S(1)} %get-tuple-element.10), channel_id=1, source_target_pairs={{0,1},{1,0},{2,3},{3,2},{4,5},{5,4},{6,7},{7,6},{8,9},{9,8},{10,11... | collective-permute-start | bytes 307208 | tf_op jit(solution)/shard_map/ppermute | solution.py:428
  19.3 2.6 %collective-permute-start.1 = (bf16[80,640]{1,0:T(8,128)(2,1)S(1)}, bf16[80,640]{1,0:T(8,128)(2,1)S(1)}, u32[]{:S(2)}, u32[]{:S(2)}) collective-permute-start(bf16[80,640]{1,0:T(8,128)(2,1)S(1)} %get-tuple-element.11), channel_id=1, source_target_pairs={{0,2},{1,3},{2,0},{3,1},{4,6},{5,7},{6,4},{7,5},{8,10},{9,11},{10,... | collective-permute-start | bytes 307208 | tf_op jit(solution)/shard_map/ppermute | solution.py:428
  21.9 0.1 collective-permute-start.2
  21.9 0.0 collective-permute-done.refs_1_
  21.9 3.7 %collective-permute-done.1.refs_2_ = bf16[80,640]{1,0:T(8,128)(2,1)S(1)} collective-permute-done((bf16[80,640]{1,0:T(8,128)(2,1)S(1)}, bf16[80,640]{1,0:T(8,128)(2,1)S(1)}, u32[]{:S(2)}, u32[]{:S(2)}) %collective-permute-start.1) | collective-permute-done | bytes 102432 | tf_op jit(solution)/shard_map/ppermute | solution.py:428
  25.6 1.7 %collective-permute-done.2.refs_3_ = bf16[80,640]{1,0:T(8,128)(2,1)S(1)} collective-permute-done((bf16[80,640]{1,0:T(8,128)(2,1)S(1)}, bf16[80,640]{1,0:T(8,128)(2,1)S(1)}, u32[]{:S(2)}, u32[]{:S(2)}) %collective-permute-start.2) | collective-permute-done | bytes 102432 | tf_op jit(solution)/shard_map/ppermute | solution.py:428
  27.3 0.0 copy-done.4
  27.3 0.0 copy-done.2
  27.3 0.0 copy-done.3
  27.3 0.0 copy-done.6
  27.3 2.4 %shard_map.92 = bf16[32,16,384]{2,1,0:T(8,128)(2,1)S(1)} custom-call(bf16[80,640]{1,0:T(8,128)(2,1)S(1)} %get-tuple-element.9.refs_0_, bf16[80,640]{1,0:T(8,128)(2,1)S(1)} %collective-permute-done.refs_1_, bf16[80,640]{1,0:T(8,128)(2,1)S(1)} %collective-permute-done.1.refs_2_, bf16[80,640]{1,0:T(8,128)(2,1)S(1)} %collective-permute-done.2.refs_3_, ...), custom_call_target="tpu_custom_call" | custom-call | tf_op jit(solution)/shard_map/pallas_call | solution.py:288
  29.7 18.9 %all_to_all.5.arrived = bf16[32,16,384]{2,1,0:T(8,128)(2,1)S(1)} all-to-all(bf16[32,16,384]{2,1,0:T(8,128)(2,1)S(1)} %shard_map.92), channel_id=1, replica_groups=mesh['rows'=8,'cols'=4] {'rows','cols'}, dimensions={0} | all-to-all | bytes 786432 | tf_op jit(solution)/shard_map/all_to_all | solution.py:430
  48.6 0.0 copy-done
  48.6 0.0 copy-done.1
  48.6 0.0 copy-done.5
  48.6 2.8 %shard_map.93 = f32[648,128]{1,0:T(8,128)} custom-call(bf16[32,16,384]{2,1,0:T(8,128)(2,1)S(1)} %all_to_all.5.arrived, f32[9,256]{1,0:T(8,128)S(1)} %copy-done.5, f32[9,512]{1,0:T(8,128)S(1)} %copy-done.4, bf16[256,512]{1,0:T(8,128)(2,1)S(1)} %copy-done.1, bf16[256,512]{1,0:T(8,128)(2,1)S(1)} %copy-done), custom_call_target="tpu_custom_call" | custom-call | tf_op jit(solution)/shard_map/pallas_call | solution.py:407
Async XLA Ops:
  0.0 27.3 %copy-start.4 = (f32[9,512]{1,0:T(8,128)S(1)}, f32[9,512]{1,0:T(8,128)}, u32[]{:S(2)}) copy-start(f32[9,512]{1,0:T(8,128)} %constant.15.clone.refs_5_.twiddle) | copy-start | bytes 55300
  0.0 27.3 %copy-start.2 = (bf16[256,512]{1,0:T(8,128)(2,1)S(1)}, bf16[256,512]{1,0:T(8,128)(2,1)}, u32[]{:S(2)}) copy-start(bf16[256,512]{1,0:T(8,128)(2,1)} %constant.17.clone.refs_7_) | copy-start | bytes 786436
  0.0 27.3 %copy-start.3 = (bf16[256,512]{1,0:T(8,128)(2,1)S(1)}, bf16[256,512]{1,0:T(8,128)(2,1)}, u32[]{:S(2)}) copy-start(bf16[256,512]{1,0:T(8,128)(2,1)} %constant.16.clone.refs_6_) | copy-start | bytes 786436
  0.0 27.3 %copy-start.6 = (f32[1,2304]{1,0:T(1,128)S(1)}, f32[1,2304]{1,0:T(1,128)}, u32[]{:S(2)}) copy-start(f32[1,2304]{1,0:T(1,128)} %constant.14.clone.refs_4_) | copy-start | bytes 27652
  0.0 48.5 %copy-start = (bf16[256,512]{1,0:T(8,128)(2,1)S(1)}, bf16[256,512]{1,0:T(8,128)(2,1)}, u32[]{:S(2)}) copy-start(bf16[256,512]{1,0:T(8,128)(2,1)} %constant.20.clone.low_table) | copy-start | bytes 786436
  0.0 48.5 %copy-start.1 = (bf16[256,512]{1,0:T(8,128)(2,1)S(1)}, bf16[256,512]{1,0:T(8,128)(2,1)}, u32[]{:S(2)}) copy-start(bf16[256,512]{1,0:T(8,128)(2,1)} %constant.19.clone.high_table) | copy-start | bytes 786436
  0.0 48.5 %copy-start.5 = (f32[9,256]{1,0:T(8,128)S(1)}, f32[9,256]{1,0:T(8,128)}, u32[]{:S(2)}) copy-start(f32[9,256]{1,0:T(8,128)} %constant.18.clone.weight) | copy-start | bytes 27652
  18.7 3.2 %collective-permute-start = (bf16[80,640]{1,0:T(8,128)(2,1)S(1)}, bf16[80,640]{1,0:T(8,128)(2,1)S(1)}, u32[]{:S(2)}, u32[]{:S(2)}) collective-permute-start(bf16[80,640]{1,0:T(8,128)(2,1)S(1)} %get-tuple-element.10), channel_id=1, source_target_pairs={{0,1},{1,0},{2,3},{3,2},{4,5},{5,4},{6,7},{7,6},{8,9},{9,8},{10,11... | collective-permute-start | bytes 307208 | tf_op jit(solution)/shard_map/ppermute | solution.py:428
  19.3 6.3 %collective-permute-start.1 = (bf16[80,640]{1,0:T(8,128)(2,1)S(1)}, bf16[80,640]{1,0:T(8,128)(2,1)S(1)}, u32[]{:S(2)}, u32[]{:S(2)}) collective-permute-start(bf16[80,640]{1,0:T(8,128)(2,1)S(1)} %get-tuple-element.11), channel_id=1, source_target_pairs={{0,2},{1,3},{2,0},{3,1},{4,6},{5,7},{6,4},{7,5},{8,10},{9,11},{10,... | collective-permute-start | bytes 307208 | tf_op jit(solution)/shard_map/ppermute | solution.py:428
  21.9 5.4 %collective-permute-start.2 = (bf16[80,640]{1,0:T(8,128)(2,1)S(1)}, bf16[80,640]{1,0:T(8,128)(2,1)S(1)}, u32[]{:S(2)}, u32[]{:S(2)}) collective-permute-start(bf16[80,640]{1,0:T(8,128)(2,1)S(1)} %get-tuple-element.12), channel_id=1, source_target_pairs={{0,3},{1,2},{2,1},{3,0},{4,7},{5,6},{6,5},{7,4},{8,11},{9,10},{10,... | collective-permute-start | bytes 307208 | tf_op jit(solution)/shard_map/ppermute | solution.py:428

commit v5 on v4

--- a/solution.py
+++ b/solution.py
@@ -94,7 +94,7 @@
 def cut_kernel(shape, field, *refs):
     outs, refs = refs[: shape[-2]], refs[shape[-2] :]
     raw, arrived, band_rows, band_cols, total, cut, ordered, coded = refs
-    taps, chunks, groups, block_outs, fold, owners, own_rows = shape
+    taps, chunks, merged, groups, block_outs, fold, owners, own_rows = shape
     block_rows = raw.shape[1]
 
     def copy(chunk):
@@ -104,11 +104,9 @@
     for chunk in range(chunks):
         copy(chunk).start()
     total[...] = jnp.zeros_like(total)
-    shape_rows = (band_rows.shape[0], block_rows)
-    ids = lax.broadcasted_iota(jnp.int32, shape_rows, 1)
-    ids = ids - STRIDE * (lax.broadcasted_iota(jnp.int32, shape_rows, 0) - ROW_MARGIN) + REACH
-    rows_band = band(taps, ids).astype(jnp.bfloat16)
-    band_rows[...] = jnp.concatenate([rows_band, rows_band], axis=1)
+    ids = lax.broadcasted_iota(jnp.int32, band_rows.shape, 1)
+    ids = ids - STRIDE * (lax.broadcasted_iota(jnp.int32, band_rows.shape, 0) - ROW_MARGIN) + REACH
+    band_rows[...] = band(taps, ids).astype(jnp.bfloat16)
     shape_8 = (8, band_cols.shape[1])
     ids = lax.broadcasted_iota(jnp.int32, shape_8, 0)
     ids = ids - STRIDE * (lax.broadcasted_iota(jnp.int32, shape_8, 1) - HALO_OUTS) + REACH
@@ -136,16 +134,22 @@
             code = encode(joined[place], scale)
             cut[place, rows, :] = jnp.where(last, scale, code) if place == places - 1 else code
 
-    def step(chunk, carry):
-        copy(chunk).wait()
-        begin = pl.multiple_of(chunk * block_outs, 8)
-        rows = pl.ds(begin, band_rows.shape[0])
+    def step(turn, carry):
+        for part in range(merged):
+            copy(turn * merged + part).wait()
+        stacked = [
+            raw[turn * merged + part, :, group * GROUP_COLS : (group + 1) * GROUP_COLS]
+            for group in range(groups)
+            for part in range(merged)
+        ]
+        high, low = split(dot(jnp.concatenate(stacked, axis=0), band_cols[...]))
+        rows = pl.ds(pl.multiple_of(turn * merged * block_outs, 8), band_rows.shape[0])
         for group in range(groups):
-            high, low = split(dot(raw[chunk, :, group * GROUP_COLS : (group + 1) * GROUP_COLS], band_cols[...]))
-            total[group, rows, :] += dot(band_rows[...], jnp.concatenate([high, low], axis=0))
+            own = slice(group * merged * block_rows, (group + 1) * merged * block_rows)
+            total[group, rows, :] += dot(band_rows[...], high[own]) + dot(band_rows[...], low[own])
         return carry
 
-    lax.fori_loop(0, chunks, step, 0)
+    lax.fori_loop(0, chunks // merged, step, 0)
     finish(0, owners * own_rows + 2 * ROW_MARGIN)
     used = own_rows + 8
     sub = lax.broadcasted_iota(jnp.int32, (8, LANES), 0)
@@ -172,14 +176,15 @@
     _, raw_rows, raw_cols = field.shape
     block_rows = next(size for size in (256, 192, 128, 64) if raw_rows % size == 0)
     chunks = raw_rows // block_rows
+    merged = 3 if chunks % 3 == 0 else 1
     groups = raw_cols // GROUP_COLS
     block_outs = block_rows // STRIDE
     own_rows = raw_rows // STRIDE // owners
-    span = block_outs + 2 * ROW_MARGIN
+    span = merged * block_outs + 2 * ROW_MARGIN
     count_rows = raw_rows // STRIDE + 2 * ROW_MARGIN
     out_cols = ceil_to(raw_cols // STRIDE + 2 * HALO_OUTS, LANES)
     taps = [float(tap) for tap in taps_host()]
-    shape = (taps, chunks, groups, block_outs, fold, owners, own_rows)
+    shape = (taps, chunks, merged, groups, block_outs, fold, owners, own_rows)
     out_rows = ceil_to(own_rows + 8, 16)
     return pl.pallas_call(
         functools.partial(cut_kernel, shape),
@@ -189,7 +194,7 @@
         scratch_shapes=[
             pltpu.VMEM((chunks, block_rows, raw_cols), jnp.bfloat16),
             pltpu.SemaphoreType.DMA((chunks,)),
-            pltpu.VMEM((span, 2 * block_rows), jnp.bfloat16),
+            pltpu.VMEM((span, merged * block_rows), jnp.bfloat16),
             pltpu.VMEM((GROUP_COLS, 2 * LANES), jnp.bfloat16),
             pltpu.VMEM((groups, count_rows, 2 * LANES), jnp.float32),
             pltpu.VMEM((out_cols // LANES, count_rows, LANES), jnp.float32),

time: 51.5 us -> 46.7 us (0.907)
  Pallas kernels: 23.8 us -> 19 us
    pallas_call x1, Pallas kernels: 18.7 us -> 13.9 us  [cut_filter(): pl.pallas_call(functools.partial(cut_kernel, shape), out_shape=[jax.Shape...]
where the time goes in v5:
time: 46.7 us; the launch traced here: 46.5 us
  Pallas kernels  19 us (41%)
  blocking collectives  18.9 us (40%)
  waiting for transfers between devices  5.34 us (11%)
  starting transfers between devices  3.2 us (7%)
    all_to_all x1, blocking collectives, local(): lax.all_to_all(partial, ('rows', 'cols'), split_axis=0, concat_axis=0, ti...  18.9 us
    pallas_call x1, Pallas kernels, cut_filter(): pl.pallas_call(functools.partial(cut_kernel, shape), out_shape=[jax.Shape...  13.9 us
    ppermute x3, waiting for transfers between devices, local(): grouped.append(lax.ppermute(cut[distance], 'cols', pairs))  5.34 us
    ppermute x3, starting transfers between devices, local(): grouped.append(lax.ppermute(cut[distance], 'cols', pairs))  3.2 us
    pallas_call x1, Pallas kernels, row_transform(): pl.pallas_call(functools.partial(row_kernel, shape), out_shape=jax.ShapeD...  2.77 us
    pallas_call x1, Pallas kernels, column_transform(): pl.pallas_call(functools.partial(column_kernel, (owners, rows, own_cols,...  2.37 us
  transfers between devices with their start and end apart: 3, of which 2 were waited for; matrix products, arithmetic and copies ran while one was open for 0% of the time, Pallas kernels for 0%

profile of v5, /device:TPU:0, one launch (start us, length us, event | category | flops | bytes accessed | tf_op | source)
XLA Modules:
  0.0 46.5 jit_solution(3554575102612617148)
XLA Ops:
  0.0 0.0 copy-start.4
  0.0 0.0 copy-start.2
  0.0 0.0 copy-start.3
  0.0 0.0 copy-start.6
  0.0 0.0 copy-start
  0.0 0.0 copy-start.1
  0.0 0.0 copy-start.5
  0.0 13.9 %shard_map.91 = (bf16[80,640]{1,0:T(8,128)(2,1)S(1)}, bf16[80,640]{1,0:T(8,128)(2,1)S(1)}, bf16[80,640]{1,0:T(8,128)(2,1)S(1)}, bf16[80,640]{1,0:T(8,128)(2,1)S(1)}) custom-call(bf16[1,2304,4608]{2,1,0:T(8,128)(2,1)} %field.1), custom_call_target="tpu_custom_call" | custom-call | tf_op jit(solution)/shard_map/pallas_call | solution.py:189
  13.9 0.5 %collective-permute-start = (bf16[80,640]{1,0:T(8,128)(2,1)S(1)}, bf16[80,640]{1,0:T(8,128)(2,1)S(1)}, u32[]{:S(2)}, u32[]{:S(2)}) collective-permute-start(bf16[80,640]{1,0:T(8,128)(2,1)S(1)} %get-tuple-element.10), channel_id=1, source_target_pairs={{0,1},{1,0},{2,3},{3,2},{4,5},{5,4},{6,7},{7,6},{8,9},{9,8},{10,11... | collective-permute-start | bytes 307208 | tf_op jit(solution)/shard_map/ppermute | solution.py:433
  14.5 2.6 %collective-permute-start.1 = (bf16[80,640]{1,0:T(8,128)(2,1)S(1)}, bf16[80,640]{1,0:T(8,128)(2,1)S(1)}, u32[]{:S(2)}, u32[]{:S(2)}) collective-permute-start(bf16[80,640]{1,0:T(8,128)(2,1)S(1)} %get-tuple-element.11), channel_id=1, source_target_pairs={{0,2},{1,3},{2,0},{3,1},{4,6},{5,7},{6,4},{7,5},{8,10},{9,11},{10,... | collective-permute-start | bytes 307208 | tf_op jit(solution)/shard_map/ppermute | solution.py:433
  17.1 0.1 collective-permute-start.2
  17.1 0.0 collective-permute-done.refs_1_
  17.1 3.7 %collective-permute-done.1.refs_2_ = bf16[80,640]{1,0:T(8,128)(2,1)S(1)} collective-permute-done((bf16[80,640]{1,0:T(8,128)(2,1)S(1)}, bf16[80,640]{1,0:T(8,128)(2,1)S(1)}, u32[]{:S(2)}, u32[]{:S(2)}) %collective-permute-start.1) | collective-permute-done | bytes 102432 | tf_op jit(solution)/shard_map/ppermute | solution.py:433
  20.8 1.7 %collective-permute-done.2.refs_3_ = bf16[80,640]{1,0:T(8,128)(2,1)S(1)} collective-permute-done((bf16[80,640]{1,0:T(8,128)(2,1)S(1)}, bf16[80,640]{1,0:T(8,128)(2,1)S(1)}, u32[]{:S(2)}, u32[]{:S(2)}) %collective-permute-start.2) | collective-permute-done | bytes 102432 | tf_op jit(solution)/shard_map/ppermute | solution.py:433
  22.5 0.0 copy-done.4
  22.5 0.0 copy-done.2
  22.5 0.0 copy-done.3
  22.5 0.0 copy-done.6
  22.5 2.4 %shard_map.92 = bf16[32,16,384]{2,1,0:T(8,128)(2,1)S(1)} custom-call(bf16[80,640]{1,0:T(8,128)(2,1)S(1)} %get-tuple-element.9.refs_0_, bf16[80,640]{1,0:T(8,128)(2,1)S(1)} %collective-permute-done.refs_1_, bf16[80,640]{1,0:T(8,128)(2,1)S(1)} %collective-permute-done.1.refs_2_, bf16[80,640]{1,0:T(8,128)(2,1)S(1)} %collective-permute-done.2.refs_3_, ...), custom_call_target="tpu_custom_call" | custom-call | tf_op jit(solution)/shard_map/pallas_call | solution.py:293
  24.9 18.9 %all_to_all.5.arrived = bf16[32,16,384]{2,1,0:T(8,128)(2,1)S(1)} all-to-all(bf16[32,16,384]{2,1,0:T(8,128)(2,1)S(1)} %shard_map.92), channel_id=1, replica_groups=mesh['rows'=8,'cols'=4] {'rows','cols'}, dimensions={0} | all-to-all | bytes 786432 | tf_op jit(solution)/shard_map/all_to_all | solution.py:435
  43.8 0.0 copy-done
  43.8 0.0 copy-done.1
  43.8 0.0 copy-done.5
  43.8 2.8 %shard_map.93 = f32[648,128]{1,0:T(8,128)} custom-call(bf16[32,16,384]{2,1,0:T(8,128)(2,1)S(1)} %all_to_all.5.arrived, f32[9,256]{1,0:T(8,128)S(1)} %copy-done.5, f32[9,512]{1,0:T(8,128)S(1)} %copy-done.4, bf16[256,512]{1,0:T(8,128)(2,1)S(1)} %copy-done.1, bf16[256,512]{1,0:T(8,128)(2,1)S(1)} %copy-done), custom_call_target="tpu_custom_call" | custom-call | tf_op jit(solution)/shard_map/pallas_call | solution.py:412
Async XLA Ops:
  0.0 22.5 %copy-start.4 = (f32[9,512]{1,0:T(8,128)S(1)}, f32[9,512]{1,0:T(8,128)}, u32[]{:S(2)}) copy-start(f32[9,512]{1,0:T(8,128)} %constant.15.clone.refs_5_.twiddle) | copy-start | bytes 55300
  0.0 22.5 %copy-start.2 = (bf16[256,512]{1,0:T(8,128)(2,1)S(1)}, bf16[256,512]{1,0:T(8,128)(2,1)}, u32[]{:S(2)}) copy-start(bf16[256,512]{1,0:T(8,128)(2,1)} %constant.17.clone.refs_7_) | copy-start | bytes 786436
  0.0 22.5 %copy-start.3 = (bf16[256,512]{1,0:T(8,128)(2,1)S(1)}, bf16[256,512]{1,0:T(8,128)(2,1)}, u32[]{:S(2)}) copy-start(bf16[256,512]{1,0:T(8,128)(2,1)} %constant.16.clone.refs_6_) | copy-start | bytes 786436
  0.0 22.5 %copy-start.6 = (f32[1,2304]{1,0:T(1,128)S(1)}, f32[1,2304]{1,0:T(1,128)}, u32[]{:S(2)}) copy-start(f32[1,2304]{1,0:T(1,128)} %constant.14.clone.refs_4_) | copy-start | bytes 27652
  0.0 43.8 %copy-start = (bf16[256,512]{1,0:T(8,128)(2,1)S(1)}, bf16[256,512]{1,0:T(8,128)(2,1)}, u32[]{:S(2)}) copy-start(bf16[256,512]{1,0:T(8,128)(2,1)} %constant.20.clone.low_table) | copy-start | bytes 786436
  0.0 43.8 %copy-start.1 = (bf16[256,512]{1,0:T(8,128)(2,1)S(1)}, bf16[256,512]{1,0:T(8,128)(2,1)}, u32[]{:S(2)}) copy-start(bf16[256,512]{1,0:T(8,128)(2,1)} %constant.19.clone.high_table) | copy-start | bytes 786436
  0.0 43.7 %copy-start.5 = (f32[9,256]{1,0:T(8,128)S(1)}, f32[9,256]{1,0:T(8,128)}, u32[]{:S(2)}) copy-start(f32[9,256]{1,0:T(8,128)} %constant.18.clone.weight) | copy-start | bytes 27652
  13.9 3.2 %collective-permute-start = (bf16[80,640]{1,0:T(8,128)(2,1)S(1)}, bf16[80,640]{1,0:T(8,128)(2,1)S(1)}, u32[]{:S(2)}, u32[]{:S(2)}) collective-permute-start(bf16[80,640]{1,0:T(8,128)(2,1)S(1)} %get-tuple-element.10), channel_id=1, source_target_pairs={{0,1},{1,0},{2,3},{3,2},{4,5},{5,4},{6,7},{7,6},{8,9},{9,8},{10,11... | collective-permute-start | bytes 307208 | tf_op jit(solution)/shard_map/ppermute | solution.py:433
  14.5 6.3 %collective-permute-start.1 = (bf16[80,640]{1,0:T(8,128)(2,1)S(1)}, bf16[80,640]{1,0:T(8,128)(2,1)S(1)}, u32[]{:S(2)}, u32[]{:S(2)}) collective-permute-start(bf16[80,640]{1,0:T(8,128)(2,1)S(1)} %get-tuple-element.11), channel_id=1, source_target_pairs={{0,2},{1,3},{2,0},{3,1},{4,6},{5,7},{6,4},{7,5},{8,10},{9,11},{10,... | collective-permute-start | bytes 307208 | tf_op jit(solution)/shard_map/ppermute | solution.py:433
  17.1 5.4 %collective-permute-start.2 = (bf16[80,640]{1,0:T(8,128)(2,1)S(1)}, bf16[80,640]{1,0:T(8,128)(2,1)S(1)}, u32[]{:S(2)}, u32[]{:S(2)}) collective-permute-start(bf16[80,640]{1,0:T(8,128)(2,1)S(1)} %get-tuple-element.12), channel_id=1, source_target_pairs={{0,3},{1,2},{2,1},{3,0},{4,7},{5,6},{6,5},{7,4},{8,11},{9,10},{10,... | collective-permute-start | bytes 307208 | tf_op jit(solution)/shard_map/ppermute | solution.py:433

commit v6 on v5

--- a/solution.py
+++ b/solution.py
@@ -176,7 +176,7 @@
     _, raw_rows, raw_cols = field.shape
     block_rows = next(size for size in (256, 192, 128, 64) if raw_rows % size == 0)
     chunks = raw_rows // block_rows
-    merged = 3 if chunks % 3 == 0 else 1
+    merged = 1
     groups = raw_cols // GROUP_COLS
     block_outs = block_rows // STRIDE
     own_rows = raw_rows // STRIDE // owners

time: 46.7 us -> 45 us (0.964)
  Pallas kernels: 19 us -> 17.4 us
    pallas_call x1, Pallas kernels: 13.9 us -> 12.2 us  [cut_filter(): pl.pallas_call(functools.partial(cut_kernel, shape), out_shape=[jax.Shape...]
where the time goes in v6:
time: 45 us; the launch traced here: 44.9 us
  blocking collectives  18.9 us (42%)
  Pallas kernels  17.4 us (39%)
  waiting for transfers between devices  5.34 us (12%)
  starting transfers between devices  3.2 us (7%)
    all_to_all x1, blocking collectives, local(): lax.all_to_all(partial, ('rows', 'cols'), split_axis=0, concat_axis=0, ti...  18.9 us
    pallas_call x1, Pallas kernels, cut_filter(): pl.pallas_call(functools.partial(cut_kernel, shape), out_shape=[jax.Shape...  12.2 us
    ppermute x3, waiting for transfers between devices, local(): grouped.append(lax.ppermute(cut[distance], 'cols', pairs))  5.34 us
    ppermute x3, starting transfers between devices, local(): grouped.append(lax.ppermute(cut[distance], 'cols', pairs))  3.2 us
    pallas_call x1, Pallas kernels, row_transform(): pl.pallas_call(functools.partial(row_kernel, shape), out_shape=jax.ShapeD...  2.77 us
    pallas_call x1, Pallas kernels, column_transform(): pl.pallas_call(functools.partial(column_kernel, (owners, rows, own_cols,...  2.37 us
  transfers between devices with their start and end apart: 3, of which 2 were waited for; matrix products, arithmetic and copies ran while one was open for 0% of the time, Pallas kernels for 0%

profile of v6, /device:TPU:0, one launch (start us, length us, event | category | flops | bytes accessed | tf_op | source)
XLA Modules:
  0.0 44.9 jit_solution(7390268701102300274)
XLA Ops:
  0.0 0.0 copy-start.4
  0.0 0.0 copy-start.2
  0.0 0.0 copy-start.3
  0.0 0.0 copy-start.6
  0.0 0.0 copy-start
  0.0 0.0 copy-start.1
  0.0 0.0 copy-start.5
  0.0 12.2 %shard_map.91 = (bf16[80,640]{1,0:T(8,128)(2,1)S(1)}, bf16[80,640]{1,0:T(8,128)(2,1)S(1)}, bf16[80,640]{1,0:T(8,128)(2,1)S(1)}, bf16[80,640]{1,0:T(8,128)(2,1)S(1)}) custom-call(bf16[1,2304,4608]{2,1,0:T(8,128)(2,1)} %field.1), custom_call_target="tpu_custom_call" | custom-call | tf_op jit(solution)/shard_map/pallas_call | solution.py:189
  12.3 0.5 %collective-permute-start = (bf16[80,640]{1,0:T(8,128)(2,1)S(1)}, bf16[80,640]{1,0:T(8,128)(2,1)S(1)}, u32[]{:S(2)}, u32[]{:S(2)}) collective-permute-start(bf16[80,640]{1,0:T(8,128)(2,1)S(1)} %get-tuple-element.10), channel_id=1, source_target_pairs={{0,1},{1,0},{2,3},{3,2},{4,5},{5,4},{6,7},{7,6},{8,9},{9,8},{10,11... | collective-permute-start | bytes 307208 | tf_op jit(solution)/shard_map/ppermute | solution.py:433
  12.8 2.6 %collective-permute-start.1 = (bf16[80,640]{1,0:T(8,128)(2,1)S(1)}, bf16[80,640]{1,0:T(8,128)(2,1)S(1)}, u32[]{:S(2)}, u32[]{:S(2)}) collective-permute-start(bf16[80,640]{1,0:T(8,128)(2,1)S(1)} %get-tuple-element.11), channel_id=1, source_target_pairs={{0,2},{1,3},{2,0},{3,1},{4,6},{5,7},{6,4},{7,5},{8,10},{9,11},{10,... | collective-permute-start | bytes 307208 | tf_op jit(solution)/shard_map/ppermute | solution.py:433
  15.4 0.1 collective-permute-start.2
  15.5 0.0 collective-permute-done.refs_1_
  15.5 3.7 %collective-permute-done.1.refs_2_ = bf16[80,640]{1,0:T(8,128)(2,1)S(1)} collective-permute-done((bf16[80,640]{1,0:T(8,128)(2,1)S(1)}, bf16[80,640]{1,0:T(8,128)(2,1)S(1)}, u32[]{:S(2)}, u32[]{:S(2)}) %collective-permute-start.1) | collective-permute-done | bytes 102432 | tf_op jit(solution)/shard_map/ppermute | solution.py:433
  19.1 1.7 %collective-permute-done.2.refs_3_ = bf16[80,640]{1,0:T(8,128)(2,1)S(1)} collective-permute-done((bf16[80,640]{1,0:T(8,128)(2,1)S(1)}, bf16[80,640]{1,0:T(8,128)(2,1)S(1)}, u32[]{:S(2)}, u32[]{:S(2)}) %collective-permute-start.2) | collective-permute-done | bytes 102432 | tf_op jit(solution)/shard_map/ppermute | solution.py:433
  20.8 0.0 copy-done.4
  20.8 0.0 copy-done.2
  20.8 0.0 copy-done.3
  20.8 0.0 copy-done.6
  20.8 2.4 %shard_map.92 = bf16[32,16,384]{2,1,0:T(8,128)(2,1)S(1)} custom-call(bf16[80,640]{1,0:T(8,128)(2,1)S(1)} %get-tuple-element.9.refs_0_, bf16[80,640]{1,0:T(8,128)(2,1)S(1)} %collective-permute-done.refs_1_, bf16[80,640]{1,0:T(8,128)(2,1)S(1)} %collective-permute-done.1.refs_2_, bf16[80,640]{1,0:T(8,128)(2,1)S(1)} %collective-permute-done.2.refs_3_, ...), custom_call_target="tpu_custom_call" | custom-call | tf_op jit(solution)/shard_map/pallas_call | solution.py:293
  23.2 18.9 %all_to_all.5.arrived = bf16[32,16,384]{2,1,0:T(8,128)(2,1)S(1)} all-to-all(bf16[32,16,384]{2,1,0:T(8,128)(2,1)S(1)} %shard_map.92), channel_id=1, replica_groups=mesh['rows'=8,'cols'=4] {'rows','cols'}, dimensions={0} | all-to-all | bytes 786432 | tf_op jit(solution)/shard_map/all_to_all | solution.py:435
  42.1 0.0 copy-done
  42.1 0.0 copy-done.1
  42.1 0.0 copy-done.5
  42.1 2.8 %shard_map.93 = f32[648,128]{1,0:T(8,128)} custom-call(bf16[32,16,384]{2,1,0:T(8,128)(2,1)S(1)} %all_to_all.5.arrived, f32[9,256]{1,0:T(8,128)S(1)} %copy-done.5, f32[9,512]{1,0:T(8,128)S(1)} %copy-done.4, bf16[256,512]{1,0:T(8,128)(2,1)S(1)} %copy-done.1, bf16[256,512]{1,0:T(8,128)(2,1)S(1)} %copy-done), custom_call_target="tpu_custom_call" | custom-call | tf_op jit(solution)/shard_map/pallas_call | solution.py:412
Async XLA Ops:
  0.0 20.8 %copy-start.4 = (f32[9,512]{1,0:T(8,128)S(1)}, f32[9,512]{1,0:T(8,128)}, u32[]{:S(2)}) copy-start(f32[9,512]{1,0:T(8,128)} %constant.15.clone.refs_5_.twiddle) | copy-start | bytes 55300
  0.0 20.8 %copy-start.2 = (bf16[256,512]{1,0:T(8,128)(2,1)S(1)}, bf16[256,512]{1,0:T(8,128)(2,1)}, u32[]{:S(2)}) copy-start(bf16[256,512]{1,0:T(8,128)(2,1)} %constant.17.clone.refs_7_) | copy-start | bytes 786436
  0.0 20.8 %copy-start.3 = (bf16[256,512]{1,0:T(8,128)(2,1)S(1)}, bf16[256,512]{1,0:T(8,128)(2,1)}, u32[]{:S(2)}) copy-start(bf16[256,512]{1,0:T(8,128)(2,1)} %constant.16.clone.refs_6_) | copy-start | bytes 786436
  0.0 20.8 %copy-start.6 = (f32[1,2304]{1,0:T(1,128)S(1)}, f32[1,2304]{1,0:T(1,128)}, u32[]{:S(2)}) copy-start(f32[1,2304]{1,0:T(1,128)} %constant.14.clone.refs_4_) | copy-start | bytes 27652
  0.0 42.1 %copy-start = (bf16[256,512]{1,0:T(8,128)(2,1)S(1)}, bf16[256,512]{1,0:T(8,128)(2,1)}, u32[]{:S(2)}) copy-start(bf16[256,512]{1,0:T(8,128)(2,1)} %constant.20.clone.low_table) | copy-start | bytes 786436
  0.0 42.1 %copy-start.1 = (bf16[256,512]{1,0:T(8,128)(2,1)S(1)}, bf16[256,512]{1,0:T(8,128)(2,1)}, u32[]{:S(2)}) copy-start(bf16[256,512]{1,0:T(8,128)(2,1)} %constant.19.clone.high_table) | copy-start | bytes 786436
  0.0 42.1 %copy-start.5 = (f32[9,256]{1,0:T(8,128)S(1)}, f32[9,256]{1,0:T(8,128)}, u32[]{:S(2)}) copy-start(f32[9,256]{1,0:T(8,128)} %constant.18.clone.weight) | copy-start | bytes 27652
  12.3 3.2 %collective-permute-start = (bf16[80,640]{1,0:T(8,128)(2,1)S(1)}, bf16[80,640]{1,0:T(8,128)(2,1)S(1)}, u32[]{:S(2)}, u32[]{:S(2)}) collective-permute-start(bf16[80,640]{1,0:T(8,128)(2,1)S(1)} %get-tuple-element.10), channel_id=1, source_target_pairs={{0,1},{1,0},{2,3},{3,2},{4,5},{5,4},{6,7},{7,6},{8,9},{9,8},{10,11... | collective-permute-start | bytes 307208 | tf_op jit(solution)/shard_map/ppermute | solution.py:433
  12.8 6.3 %collective-permute-start.1 = (bf16[80,640]{1,0:T(8,128)(2,1)S(1)}, bf16[80,640]{1,0:T(8,128)(2,1)S(1)}, u32[]{:S(2)}, u32[]{:S(2)}) collective-permute-start(bf16[80,640]{1,0:T(8,128)(2,1)S(1)} %get-tuple-element.11), channel_id=1, source_target_pairs={{0,2},{1,3},{2,0},{3,1},{4,6},{5,7},{6,4},{7,5},{8,10},{9,11},{10,... | collective-permute-start | bytes 307208 | tf_op jit(solution)/shard_map/ppermute | solution.py:433
  15.4 5.4 %collective-permute-start.2 = (bf16[80,640]{1,0:T(8,128)(2,1)S(1)}, bf16[80,640]{1,0:T(8,128)(2,1)S(1)}, u32[]{:S(2)}, u32[]{:S(2)}) collective-permute-start(bf16[80,640]{1,0:T(8,128)(2,1)S(1)} %get-tuple-element.12), channel_id=1, source_target_pairs={{0,3},{1,2},{2,1},{3,0},{4,7},{5,6},{6,5},{7,4},{8,11},{9,10},{10,... | collective-permute-start | bytes 307208 | tf_op jit(solution)/shard_map/ppermute | solution.py:433

commit v7 on v6

--- a/solution.py
+++ b/solution.py
@@ -208,19 +208,20 @@
 def column_kernel(shape, *refs):
     owners, rows, own_cols, fold = shape
     blocks, refs = refs[:owners], refs[owners:]
-    weight, twiddle, high_table, low_table, out, joined, high_rows, low_rows = refs
+    weight, twiddle, table, out, held, joined, high_rows, low_rows = refs
     own_col = lax.axis_index("cols")
     joined[...] = jnp.zeros_like(joined)
     width = blocks[0].shape[1]
     inside = lax.broadcasted_iota(jnp.int32, (rows, width), 1) < own_cols + 2 * HALO_OUTS
     for distance in range(owners):
-        first = LANES + own_cols * (own_col ^ distance) - HALO_OUTS
         code = blocks[distance][...].astype(jnp.float32)
         value = decode(code, code[:, width - 1 :])
-        value = jnp.where(inside, value, 0.0)
-        block = jnp.concatenate([value, jnp.zeros((rows, LANES), jnp.float32)], axis=1)
-        base = pl.multiple_of(first // LANES * LANES, LANES)
-        joined[:, pl.ds(base, width + LANES)] += pltpu.roll(block, first % LANES, 1)
+        held[own_col ^ distance] = jnp.where(inside, value, 0.0)
+    for owner in range(owners):
+        first = LANES + own_cols * owner - HALO_OUTS
+        block = jnp.concatenate([held[owner], jnp.zeros((rows, LANES), jnp.float32)], axis=1)
+        base = first // LANES * LANES
+        joined[:, base : base + width + LANES] += pltpu.roll(block, first - base, 1)
     points = [
         joined[:, LANES + INNER * i : LANES + INNER * (i + 1)] * weight[:, INNER * i : INNER * (i + 1)]
         for i in range(fold)
@@ -256,9 +257,8 @@
             imag = term if imag is None else imag + term
         turned(freq, real, imag)
         turned(fold - freq, real, -imag)
-    result = dot_nt(high_table[...], high_rows[...])
-    result += dot_nt(high_table[...], low_rows[...])
-    result += dot_nt(low_table[...], high_rows[...])
+    both = dot_nt(table[...], high_rows[...])
+    result = both[:INNER] + both[INNER:] + dot_nt(table[:INNER, :], low_rows[...])
     scale = row_scale(result)
     code = encode(result, scale)
     lane = lax.broadcasted_iota(jnp.int32, code.shape, 1)
@@ -287,19 +287,20 @@
         ]
     )
     table = table.reshape(2, devices, per_device, 2 * INNER).transpose(1, 0, 2, 3).reshape(INNER, 2 * INNER)
-    high_table, low_table = split_host(table)
+    table = np.concatenate(split_host(table), axis=0)
     pieces = max(16 // (2 * per_device), 1)
     lanes = ceil_to(fold * rows + 1, pieces * LANES)
     return pl.pallas_call(
         functools.partial(column_kernel, (owners, rows, own_cols, fold)),
         out_shape=jax.ShapeDtypeStruct((devices, pieces * 2 * per_device, lanes // pieces), jnp.bfloat16),
         scratch_shapes=[
+            pltpu.VMEM((owners, rows, width), jnp.float32),
             pltpu.VMEM((rows, length + 2 * LANES), jnp.float32),
             pltpu.VMEM((lanes, 2 * INNER), jnp.bfloat16),
             pltpu.VMEM((lanes, 2 * INNER), jnp.bfloat16),
         ],
         compiler_params=pltpu.CompilerParams(vmem_limit_bytes=48 * 2**20),
-    )(*blocks, jnp.asarray(taper_host(length)[None, :]), jnp.asarray(twiddle), jnp.asarray(high_table), jnp.asarray(low_table))
+    )(*blocks, jnp.asarray(taper_host(length)[None, :]), jnp.asarray(twiddle), jnp.asarray(table))
 
 
 def row_kernel(shape, arrived, weight, twiddle, high_table, low_table, out, blocks, spread, folded):
@@ -361,7 +362,8 @@
             )
 
     high, low = split(folded[...])
-    result = dot(high, high_table[...]) + dot(low, high_table[...]) + dot(high, low_table[...])
+    both = dot(jnp.concatenate([high, low], axis=0), high_table[...])
+    result = both[: high.shape[0]] + both[high.shape[0] :] + dot(high, low_table[...])
     for freq in range(fold):
         points = []
         for point in range(fold):
@@ -427,10 +429,10 @@
     length = field.shape[1] // STRIDE * lax.axis_size("rows")
     fold = length // INNER
     cut = cut_filter(field, owners, fold)
-    grouped = [cut[0]]
-    for distance in range(1, owners):
+    grouped = [cut[0]] * owners
+    for distance in reversed(range(1, owners)):
         pairs = [(col, col ^ distance) for col in range(owners)]
-        grouped.append(lax.ppermute(cut[distance], "cols", pairs))
+        grouped[distance] = lax.ppermute(cut[distance], "cols", pairs)
     partial = column_transform(grouped, length, devices)
     arrived = lax.all_to_all(partial, ("rows", "cols"), split_axis=0, concat_axis=0, tiled=True)
     return row_transform(arrived, length, grouped[0].shape[0]).reshape(1, -1, length)

time: 45 us -> 44.9 us (level)
  no operation moved by 1% of the time
where the time goes in v7:
time: 44.9 us; the launch traced here: 44.7 us
  blocking collectives  18.9 us (42%)
  Pallas kernels  17.2 us (38%)
  waiting for transfers between devices  5.34 us (12%)
  starting transfers between devices  3.2 us (7%)
    all_to_all x1, blocking collectives, local(): lax.all_to_all(partial, ('rows', 'cols'), split_axis=0, concat_axis=0, ti...  18.9 us
    pallas_call x1, Pallas kernels, cut_filter(): pl.pallas_call(functools.partial(cut_kernel, shape), out_shape=[jax.Shape...  12.2 us
    ppermute x3, waiting for transfers between devices, local(): grouped[distance] = lax.ppermute(cut[distance], 'cols', pairs)  5.34 us
    ppermute x3, starting transfers between devices, local(): grouped[distance] = lax.ppermute(cut[distance], 'cols', pairs)  3.2 us
    pallas_call x1, Pallas kernels, row_transform(): pl.pallas_call(functools.partial(row_kernel, shape), out_shape=jax.ShapeD...  2.81 us
    pallas_call x1, Pallas kernels, column_transform(): pl.pallas_call(functools.partial(column_kernel, (owners, rows, own_cols,...  2.22 us
  transfers between devices with their start and end apart: 3, of which 2 were waited for; matrix products, arithmetic and copies ran while one was open for 0% of the time, Pallas kernels for 0%

profile of v7, /device:TPU:0, one launch (start us, length us, event | category | flops | bytes accessed | tf_op | source)
XLA Modules:
  0.0 44.7 jit_solution(15424794960118550471)
XLA Ops:
  0.0 0.0 copy-start.3
  0.0 0.0 copy-start
  0.0 0.0 copy-start.5
  0.0 0.0 copy-start.1
  0.0 0.0 copy-start.2
  0.0 0.0 copy-start.4
  0.0 12.2 %shard_map.82 = (bf16[80,640]{1,0:T(8,128)(2,1)S(1)}, bf16[80,640]{1,0:T(8,128)(2,1)S(1)}, bf16[80,640]{1,0:T(8,128)(2,1)S(1)}, bf16[80,640]{1,0:T(8,128)(2,1)S(1)}) custom-call(bf16[1,2304,4608]{2,1,0:T(8,128)(2,1)} %field.1), custom_call_target="tpu_custom_call" | custom-call | tf_op jit(solution)/shard_map/pallas_call | solution.py:189
  12.2 0.5 %collective-permute-start = (bf16[80,640]{1,0:T(8,128)(2,1)S(1)}, bf16[80,640]{1,0:T(8,128)(2,1)S(1)}, u32[]{:S(2)}, u32[]{:S(2)}) collective-permute-start(bf16[80,640]{1,0:T(8,128)(2,1)S(1)} %get-tuple-element.10), channel_id=1, source_target_pairs={{0,1},{1,0},{2,3},{3,2},{4,5},{5,4},{6,7},{7,6},{8,9},{9,8},{10,11... | collective-permute-start | bytes 307208 | tf_op jit(solution)/shard_map/ppermute | solution.py:435
  12.8 2.6 %collective-permute-start.1 = (bf16[80,640]{1,0:T(8,128)(2,1)S(1)}, bf16[80,640]{1,0:T(8,128)(2,1)S(1)}, u32[]{:S(2)}, u32[]{:S(2)}) collective-permute-start(bf16[80,640]{1,0:T(8,128)(2,1)S(1)} %get-tuple-element.11), channel_id=1, source_target_pairs={{0,2},{1,3},{2,0},{3,1},{4,6},{5,7},{6,4},{7,5},{8,10},{9,11},{10,... | collective-permute-start | bytes 307208 | tf_op jit(solution)/shard_map/ppermute | solution.py:435
  15.4 0.1 collective-permute-start.2
  15.4 0.0 collective-permute-done.refs_1_
  15.4 3.7 %collective-permute-done.1.refs_2_ = bf16[80,640]{1,0:T(8,128)(2,1)S(1)} collective-permute-done((bf16[80,640]{1,0:T(8,128)(2,1)S(1)}, bf16[80,640]{1,0:T(8,128)(2,1)S(1)}, u32[]{:S(2)}, u32[]{:S(2)}) %collective-permute-start.1) | collective-permute-done | bytes 102432 | tf_op jit(solution)/shard_map/ppermute | solution.py:435
  19.1 1.7 %collective-permute-done.2.refs_3_ = bf16[80,640]{1,0:T(8,128)(2,1)S(1)} collective-permute-done((bf16[80,640]{1,0:T(8,128)(2,1)S(1)}, bf16[80,640]{1,0:T(8,128)(2,1)S(1)}, u32[]{:S(2)}, u32[]{:S(2)}) %collective-permute-start.2) | collective-permute-done | bytes 102432 | tf_op jit(solution)/shard_map/ppermute | solution.py:435
  20.8 0.0 copy-done.3
  20.8 0.0 copy-done
  20.8 0.0 copy-done.5
  20.8 2.2 %shard_map.83 = bf16[32,16,384]{2,1,0:T(8,128)(2,1)S(1)} custom-call(bf16[80,640]{1,0:T(8,128)(2,1)S(1)} %get-tuple-element.9.refs_0_, bf16[80,640]{1,0:T(8,128)(2,1)S(1)} %collective-permute-done.refs_1_, bf16[80,640]{1,0:T(8,128)(2,1)S(1)} %collective-permute-done.1.refs_2_, bf16[80,640]{1,0:T(8,128)(2,1)S(1)} %collective-permute-done.2.refs_3_, ...), custom_call_target="tpu_custom_call" | custom-call | tf_op jit(solution)/shard_map/pallas_call | solution.py:293
  23.0 18.9 %all_to_all.5.arrived = bf16[32,16,384]{2,1,0:T(8,128)(2,1)S(1)} all-to-all(bf16[32,16,384]{2,1,0:T(8,128)(2,1)S(1)} %shard_map.83), channel_id=1, replica_groups=mesh['rows'=8,'cols'=4] {'rows','cols'}, dimensions={0} | all-to-all | bytes 786432 | tf_op jit(solution)/shard_map/all_to_all | solution.py:437
  41.9 0.0 copy-done.1
  41.9 0.0 copy-done.2
  41.9 0.0 copy-done.4
  41.9 2.8 %shard_map.84 = f32[648,128]{1,0:T(8,128)} custom-call(bf16[32,16,384]{2,1,0:T(8,128)(2,1)S(1)} %all_to_all.5.arrived, f32[9,256]{1,0:T(8,128)S(1)} %copy-done.4, f32[9,512]{1,0:T(8,128)S(1)} %copy-done.3, bf16[256,512]{1,0:T(8,128)(2,1)S(1)} %copy-done.2, bf16[256,512]{1,0:T(8,128)(2,1)S(1)} %copy-done.1), custom_call_target="tpu_custom_call" | custom-call | tf_op jit(solution)/shard_map/pallas_call | solution.py:414
Async XLA Ops:
  0.0 20.8 %copy-start.3 = (f32[9,512]{1,0:T(8,128)S(1)}, f32[9,512]{1,0:T(8,128)}, u32[]{:S(2)}) copy-start(f32[9,512]{1,0:T(8,128)} %constant.13.clone.refs_5_.twiddle) | copy-start | bytes 55300
  0.0 20.8 %copy-start = (bf16[512,512]{1,0:T(8,128)(2,1)S(1)}, bf16[512,512]{1,0:T(8,128)(2,1)}, u32[]{:S(2)}) copy-start(bf16[512,512]{1,0:T(8,128)(2,1)} %constant.14.clone.refs_6_) | copy-start | bytes 1572868
  0.0 20.8 %copy-start.5 = (f32[1,2304]{1,0:T(1,128)S(1)}, f32[1,2304]{1,0:T(1,128)}, u32[]{:S(2)}) copy-start(f32[1,2304]{1,0:T(1,128)} %constant.12.clone.refs_4_) | copy-start | bytes 27652
  0.0 41.9 %copy-start.1 = (bf16[256,512]{1,0:T(8,128)(2,1)S(1)}, bf16[256,512]{1,0:T(8,128)(2,1)}, u32[]{:S(2)}) copy-start(bf16[256,512]{1,0:T(8,128)(2,1)} %constant.17.clone.low_table) | copy-start | bytes 786436
  0.0 41.9 %copy-start.2 = (bf16[256,512]{1,0:T(8,128)(2,1)S(1)}, bf16[256,512]{1,0:T(8,128)(2,1)}, u32[]{:S(2)}) copy-start(bf16[256,512]{1,0:T(8,128)(2,1)} %constant.16.clone.high_table) | copy-start | bytes 786436
  0.0 41.9 %copy-start.4 = (f32[9,256]{1,0:T(8,128)S(1)}, f32[9,256]{1,0:T(8,128)}, u32[]{:S(2)}) copy-start(f32[9,256]{1,0:T(8,128)} %constant.15.clone.weight) | copy-start | bytes 27652
  12.2 3.2 %collective-permute-start = (bf16[80,640]{1,0:T(8,128)(2,1)S(1)}, bf16[80,640]{1,0:T(8,128)(2,1)S(1)}, u32[]{:S(2)}, u32[]{:S(2)}) collective-permute-start(bf16[80,640]{1,0:T(8,128)(2,1)S(1)} %get-tuple-element.10), channel_id=1, source_target_pairs={{0,1},{1,0},{2,3},{3,2},{4,5},{5,4},{6,7},{7,6},{8,9},{9,8},{10,11... | collective-permute-start | bytes 307208 | tf_op jit(solution)/shard_map/ppermute | solution.py:435
  12.8 6.3 %collective-permute-start.1 = (bf16[80,640]{1,0:T(8,128)(2,1)S(1)}, bf16[80,640]{1,0:T(8,128)(2,1)S(1)}, u32[]{:S(2)}, u32[]{:S(2)}) collective-permute-start(bf16[80,640]{1,0:T(8,128)(2,1)S(1)} %get-tuple-element.11), channel_id=1, source_target_pairs={{0,2},{1,3},{2,0},{3,1},{4,6},{5,7},{6,4},{7,5},{8,10},{9,11},{10,... | collective-permute-start | bytes 307208 | tf_op jit(solution)/shard_map/ppermute | solution.py:435
  15.4 5.4 %collective-permute-start.2 = (bf16[80,640]{1,0:T(8,128)(2,1)S(1)}, bf16[80,640]{1,0:T(8,128)(2,1)S(1)}, u32[]{:S(2)}, u32[]{:S(2)}) collective-permute-start(bf16[80,640]{1,0:T(8,128)(2,1)S(1)} %get-tuple-element.12), channel_id=1, source_target_pairs={{0,3},{1,2},{2,1},{3,0},{4,7},{5,6},{6,5},{7,4},{8,11},{9,10},{10,... | collective-permute-start | bytes 307208 | tf_op jit(solution)/shard_map/ppermute | solution.py:435

commit v8 on v7

--- a/solution.py
+++ b/solution.py
@@ -89,6 +89,10 @@
 
 def dot_nt(left, right):
     return lax.dot_general(left, right, (((1,), (1,)), ((), ())), preferred_element_type=jnp.float32)
+
+
+def distance_of(index, owners):
+    return (owners - index) % owners
 
 
 def cut_kernel(shape, field, *refs):
@@ -147,10 +151,11 @@
         for group in range(groups):
             own = slice(group * merged * block_rows, (group + 1) * merged * block_rows)
             total[group, rows, :] += dot(band_rows[...], high[own]) + dot(band_rows[...], low[own])
+        finish(pl.multiple_of(turn * merged * block_outs, 8), merged * block_outs)
         return carry
 
     lax.fori_loop(0, chunks // merged, step, 0)
-    finish(0, owners * own_rows + 2 * ROW_MARGIN)
+    finish(owners * own_rows, 2 * ROW_MARGIN)
     used = own_rows + 8
     sub = lax.broadcasted_iota(jnp.int32, (8, LANES), 0)
     if ordered.shape[0] > used:
@@ -168,8 +173,8 @@
             ordered[own_rows:used, lanes] = jnp.where(sub == 0, row, NONE_CODE)
         coded[owner] = ordered[...].astype(jnp.bfloat16)
     own_col = lax.axis_index("cols")
-    for distance in range(owners):
-        outs[distance][...] = coded[own_col ^ distance]
+    for index, out in enumerate(outs):
+        out[...] = coded[own_col ^ distance_of(index, owners)]
 
 
 def cut_filter(field, owners, fold):
@@ -213,10 +218,10 @@
     joined[...] = jnp.zeros_like(joined)
     width = blocks[0].shape[1]
     inside = lax.broadcasted_iota(jnp.int32, (rows, width), 1) < own_cols + 2 * HALO_OUTS
-    for distance in range(owners):
-        code = blocks[distance][...].astype(jnp.float32)
+    for index, block in enumerate(blocks):
+        code = block[...].astype(jnp.float32)
         value = decode(code, code[:, width - 1 :])
-        held[own_col ^ distance] = jnp.where(inside, value, 0.0)
+        held[own_col ^ distance_of(index, owners)] = jnp.where(inside, value, 0.0)
     for owner in range(owners):
         first = LANES + own_cols * owner - HALO_OUTS
         block = jnp.concatenate([held[owner], jnp.zeros((rows, LANES), jnp.float32)], axis=1)
@@ -429,10 +434,10 @@
     length = field.shape[1] // STRIDE * lax.axis_size("rows")
     fold = length // INNER
     cut = cut_filter(field, owners, fold)
-    grouped = [cut[0]] * owners
-    for distance in reversed(range(1, owners)):
-        pairs = [(col, col ^ distance) for col in range(owners)]
-        grouped[distance] = lax.ppermute(cut[distance], "cols", pairs)
+    grouped = [cut[0]]
+    for index in range(1, owners):
+        pairs = [(col, col ^ distance_of(index, owners)) for col in range(owners)]
+        grouped.append(lax.ppermute(cut[index], "cols", pairs))
     partial = column_transform(grouped, length, devices)
     arrived = lax.all_to_all(partial, ("rows", "cols"), split_axis=0, concat_axis=0, tiled=True)
     return row_transform(arrived, length, grouped[0].shape[0]).reshape(1, -1, length)

time: 44.9 us -> 45.9 us (1.022)
  Pallas kernels: 17.2 us -> 18 us
  blocking collectives: 18.9 us -> 19.6 us
    pallas_call x1, Pallas kernels: 12.2 us -> 12.9 us  [cut_filter(): pl.pallas_call(functools.partial(cut_kernel, shape), out_shape=[jax.Shape...]
    all_to_all x1, blocking collectives: 18.9 us -> 19.6 us  [local(): lax.all_to_all(partial, ('rows', 'cols'), split_axis=0, concat_axis=0, ti...]
where the time goes in v8:
time: 45.9 us; the launch traced here: 45.8 us
  blocking collectives  19.6 us (43%)
  Pallas kernels  18 us (39%)
  waiting for transfers between devices  4.96 us (11%)
  starting transfers between devices  3.17 us (7%)
    all_to_all x1, blocking collectives, local(): lax.all_to_all(partial, ('rows', 'cols'), split_axis=0, concat_axis=0, ti...  19.6 us
    pallas_call x1, Pallas kernels, cut_filter(): pl.pallas_call(functools.partial(cut_kernel, shape), out_shape=[jax.Shape...  12.9 us
    ppermute x3, waiting for transfers between devices, local(): grouped.append(lax.ppermute(cut[index], 'cols', pairs))  4.96 us
    ppermute x3, starting transfers between devices, local(): grouped.append(lax.ppermute(cut[index], 'cols', pairs))  3.17 us
    pallas_call x1, Pallas kernels, row_transform(): pl.pallas_call(functools.partial(row_kernel, shape), out_shape=jax.ShapeD...  2.81 us
    pallas_call x1, Pallas kernels, column_transform(): pl.pallas_call(functools.partial(column_kernel, (owners, rows, own_cols,...  2.22 us
  transfers between devices with their start and end apart: 3, of which 2 were waited for; matrix products, arithmetic and copies ran while one was open for 0% of the time, Pallas kernels for 0%

profile of v8, /device:TPU:0, one launch (start us, length us, event | category | flops | bytes accessed | tf_op | source)
XLA Modules:
  0.0 45.8 jit_solution(10305541930319965781)
XLA Ops:
  0.0 0.0 copy-start.3
  0.0 0.0 copy-start
  0.0 0.0 copy-start.5
  0.0 0.0 copy-start.1
  0.0 0.0 copy-start.2
  0.0 0.0 copy-start.4
  0.0 12.9 %shard_map.82 = (bf16[80,640]{1,0:T(8,128)(2,1)S(1)}, bf16[80,640]{1,0:T(8,128)(2,1)S(1)}, bf16[80,640]{1,0:T(8,128)(2,1)S(1)}, bf16[80,640]{1,0:T(8,128)(2,1)S(1)}) custom-call(bf16[1,2304,4608]{2,1,0:T(8,128)(2,1)} %field.1), custom_call_target="tpu_custom_call" | custom-call | tf_op jit(solution)/shard_map/pallas_call | solution.py:194
  13.0 2.5 %collective-permute-start = (bf16[80,640]{1,0:T(8,128)(2,1)S(1)}, bf16[80,640]{1,0:T(8,128)(2,1)S(1)}, u32[]{:S(2)}, u32[]{:S(2)}) collective-permute-start(bf16[80,640]{1,0:T(8,128)(2,1)S(1)} %get-tuple-element.10), channel_id=1, source_target_pairs={{0,3},{1,2},{2,1},{3,0},{4,7},{5,6},{6,5},{7,4},{8,11},{9,10},{10,... | collective-permute-start | bytes 307208 | tf_op jit(solution)/shard_map/ppermute | solution.py:440
  15.5 0.6 %collective-permute-start.1 = (bf16[80,640]{1,0:T(8,128)(2,1)S(1)}, bf16[80,640]{1,0:T(8,128)(2,1)S(1)}, u32[]{:S(2)}, u32[]{:S(2)}) collective-permute-start(bf16[80,640]{1,0:T(8,128)(2,1)S(1)} %get-tuple-element.11), channel_id=1, source_target_pairs={{0,2},{1,3},{2,0},{3,1},{4,6},{5,7},{6,4},{7,5},{8,10},{9,11},{10,... | collective-permute-start | bytes 307208 | tf_op jit(solution)/shard_map/ppermute | solution.py:440
  16.1 0.0 collective-permute-start.2
  16.2 2.6 %collective-permute-done.refs_1_ = bf16[80,640]{1,0:T(8,128)(2,1)S(1)} collective-permute-done((bf16[80,640]{1,0:T(8,128)(2,1)S(1)}, bf16[80,640]{1,0:T(8,128)(2,1)S(1)}, u32[]{:S(2)}, u32[]{:S(2)}) %collective-permute-start) | collective-permute-done | bytes 102432 | tf_op jit(solution)/shard_map/ppermute | solution.py:440
  18.7 2.4 %collective-permute-done.1.refs_2_ = bf16[80,640]{1,0:T(8,128)(2,1)S(1)} collective-permute-done((bf16[80,640]{1,0:T(8,128)(2,1)S(1)}, bf16[80,640]{1,0:T(8,128)(2,1)S(1)}, u32[]{:S(2)}, u32[]{:S(2)}) %collective-permute-start.1) | collective-permute-done | bytes 102432 | tf_op jit(solution)/shard_map/ppermute | solution.py:440
  21.1 0.0 collective-permute-done.2.refs_3_
  21.1 0.0 copy-done.3
  21.1 0.0 copy-done
  21.1 0.0 copy-done.5
  21.1 2.2 %shard_map.83 = bf16[32,16,384]{2,1,0:T(8,128)(2,1)S(1)} custom-call(bf16[80,640]{1,0:T(8,128)(2,1)S(1)} %get-tuple-element.9.refs_0_, bf16[80,640]{1,0:T(8,128)(2,1)S(1)} %collective-permute-done.refs_1_, bf16[80,640]{1,0:T(8,128)(2,1)S(1)} %collective-permute-done.1.refs_2_, bf16[80,640]{1,0:T(8,128)(2,1)S(1)} %collective-permute-done.2.refs_3_, ...), custom_call_target="tpu_custom_call" | custom-call | tf_op jit(solution)/shard_map/pallas_call | solution.py:298
  23.4 19.6 %all_to_all.5.arrived = bf16[32,16,384]{2,1,0:T(8,128)(2,1)S(1)} all-to-all(bf16[32,16,384]{2,1,0:T(8,128)(2,1)S(1)} %shard_map.83), channel_id=1, replica_groups=mesh['rows'=8,'cols'=4] {'rows','cols'}, dimensions={0} | all-to-all | bytes 786432 | tf_op jit(solution)/shard_map/all_to_all | solution.py:442
  43.0 0.0 copy-done.1
  43.0 0.0 copy-done.2
  43.0 0.0 copy-done.4
  43.0 2.8 %shard_map.84 = f32[648,128]{1,0:T(8,128)} custom-call(bf16[32,16,384]{2,1,0:T(8,128)(2,1)S(1)} %all_to_all.5.arrived, f32[9,256]{1,0:T(8,128)S(1)} %copy-done.4, f32[9,512]{1,0:T(8,128)S(1)} %copy-done.3, bf16[256,512]{1,0:T(8,128)(2,1)S(1)} %copy-done.2, bf16[256,512]{1,0:T(8,128)(2,1)S(1)} %copy-done.1), custom_call_target="tpu_custom_call" | custom-call | tf_op jit(solution)/shard_map/pallas_call | solution.py:419
Async XLA Ops:
  0.0 21.1 %copy-start.3 = (f32[9,512]{1,0:T(8,128)S(1)}, f32[9,512]{1,0:T(8,128)}, u32[]{:S(2)}) copy-start(f32[9,512]{1,0:T(8,128)} %constant.13.clone.refs_5_.twiddle) | copy-start | bytes 55300
  0.0 21.1 %copy-start = (bf16[512,512]{1,0:T(8,128)(2,1)S(1)}, bf16[512,512]{1,0:T(8,128)(2,1)}, u32[]{:S(2)}) copy-start(bf16[512,512]{1,0:T(8,128)(2,1)} %constant.14.clone.refs_6_) | copy-start | bytes 1572868
  0.0 21.1 %copy-start.5 = (f32[1,2304]{1,0:T(1,128)S(1)}, f32[1,2304]{1,0:T(1,128)}, u32[]{:S(2)}) copy-start(f32[1,2304]{1,0:T(1,128)} %constant.12.clone.refs_4_) | copy-start | bytes 27652
  0.0 43.0 %copy-start.1 = (bf16[256,512]{1,0:T(8,128)(2,1)S(1)}, bf16[256,512]{1,0:T(8,128)(2,1)}, u32[]{:S(2)}) copy-start(bf16[256,512]{1,0:T(8,128)(2,1)} %constant.17.clone.low_table) | copy-start | bytes 786436
  0.0 43.0 %copy-start.2 = (bf16[256,512]{1,0:T(8,128)(2,1)S(1)}, bf16[256,512]{1,0:T(8,128)(2,1)}, u32[]{:S(2)}) copy-start(bf16[256,512]{1,0:T(8,128)(2,1)} %constant.16.clone.high_table) | copy-start | bytes 786436
  0.0 43.0 %copy-start.4 = (f32[9,256]{1,0:T(8,128)S(1)}, f32[9,256]{1,0:T(8,128)}, u32[]{:S(2)}) copy-start(f32[9,256]{1,0:T(8,128)} %constant.15.clone.weight) | copy-start | bytes 27652
  13.0 5.8 %collective-permute-start = (bf16[80,640]{1,0:T(8,128)(2,1)S(1)}, bf16[80,640]{1,0:T(8,128)(2,1)S(1)}, u32[]{:S(2)}, u32[]{:S(2)}) collective-permute-start(bf16[80,640]{1,0:T(8,128)(2,1)S(1)} %get-tuple-element.10), channel_id=1, source_target_pairs={{0,3},{1,2},{2,1},{3,0},{4,7},{5,6},{6,5},{7,4},{8,11},{9,10},{10,... | collective-permute-start | bytes 307208 | tf_op jit(solution)/shard_map/ppermute | solution.py:440
  15.5 5.6 %collective-permute-start.1 = (bf16[80,640]{1,0:T(8,128)(2,1)S(1)}, bf16[80,640]{1,0:T(8,128)(2,1)S(1)}, u32[]{:S(2)}, u32[]{:S(2)}) collective-permute-start(bf16[80,640]{1,0:T(8,128)(2,1)S(1)} %get-tuple-element.11), channel_id=1, source_target_pairs={{0,2},{1,3},{2,0},{3,1},{4,6},{5,7},{6,4},{7,5},{8,10},{9,11},{10,... | collective-permute-start | bytes 307208 | tf_op jit(solution)/shard_map/ppermute | solution.py:440
  16.1 5.0 %collective-permute-start.2 = (bf16[80,640]{1,0:T(8,128)(2,1)S(1)}, bf16[80,640]{1,0:T(8,128)(2,1)S(1)}, u32[]{:S(2)}, u32[]{:S(2)}) collective-permute-start(bf16[80,640]{1,0:T(8,128)(2,1)S(1)} %get-tuple-element.12), channel_id=1, source_target_pairs={{0,1},{1,0},{2,3},{3,2},{4,5},{5,4},{6,7},{7,6},{8,9},{9,8},{10,11... | collective-permute-start | bytes 307208 | tf_op jit(solution)/shard_map/ppermute | solution.py:440

commit v9 on v7

--- a/solution.py
+++ b/solution.py
@@ -257,8 +257,8 @@
             imag = term if imag is None else imag + term
         turned(freq, real, imag)
         turned(fold - freq, real, -imag)
-    both = dot_nt(table[...], high_rows[...])
-    result = both[:INNER] + both[INNER:] + dot_nt(table[:INNER, :], low_rows[...])
+    both = dot(high_rows[...], table[...])
+    result = (both[:, :INNER] + both[:, INNER:] + dot(low_rows[...], table[:, :INNER])).T
     scale = row_scale(result)
     code = encode(result, scale)
     lane = lax.broadcasted_iota(jnp.int32, code.shape, 1)
@@ -287,7 +287,7 @@
         ]
     )
     table = table.reshape(2, devices, per_device, 2 * INNER).transpose(1, 0, 2, 3).reshape(INNER, 2 * INNER)
-    table = np.concatenate(split_host(table), axis=0)
+    table = np.concatenate([part.T for part in split_host(table)], axis=1)
     pieces = max(16 // (2 * per_device), 1)
     lanes = ceil_to(fold * rows + 1, pieces * LANES)
     return pl.pallas_call(

time: 44.9 us -> 44.9 us (level)
  no operation moved by 1% of the time
where the time goes in v9:
time: 44.9 us; the launch traced here: 44.7 us
  blocking collectives  18.9 us (42%)
  Pallas kernels  17.2 us (38%)
  waiting for transfers between devices  5.34 us (12%)
  starting transfers between devices  3.2 us (7%)
    all_to_all x1, blocking collectives, local(): lax.all_to_all(partial, ('rows', 'cols'), split_axis=0, concat_axis=0, ti...  18.9 us
    pallas_call x1, Pallas kernels, cut_filter(): pl.pallas_call(functools.partial(cut_kernel, shape), out_shape=[jax.Shape...  12.2 us
    ppermute x3, waiting for transfers between devices, local(): grouped[distance] = lax.ppermute(cut[distance], 'cols', pairs)  5.34 us
    ppermute x3, starting transfers between devices, local(): grouped[distance] = lax.ppermute(cut[distance], 'cols', pairs)  3.2 us
    pallas_call x1, Pallas kernels, row_transform(): pl.pallas_call(functools.partial(row_kernel, shape), out_shape=jax.ShapeD...  2.81 us
    pallas_call x1, Pallas kernels, column_transform(): pl.pallas_call(functools.partial(column_kernel, (owners, rows, own_cols,...  2.22 us
  transfers between devices with their start and end apart: 3, of which 2 were waited for; matrix products, arithmetic and copies ran while one was open for 0% of the time, Pallas kernels for 0%

profile of v9, /device:TPU:0, one launch (start us, length us, event | category | flops | bytes accessed | tf_op | source)
XLA Modules:
  0.0 44.7 jit_solution(4242288104033582690)
XLA Ops:
  0.0 0.0 copy-start.3
  0.0 0.0 copy-start
  0.0 0.0 copy-start.5
  0.0 0.0 copy-start.1
  0.0 0.0 copy-start.2
  0.0 0.0 copy-start.4
  0.0 12.2 %shard_map.82 = (bf16[80,640]{1,0:T(8,128)(2,1)S(1)}, bf16[80,640]{1,0:T(8,128)(2,1)S(1)}, bf16[80,640]{1,0:T(8,128)(2,1)S(1)}, bf16[80,640]{1,0:T(8,128)(2,1)S(1)}) custom-call(bf16[1,2304,4608]{2,1,0:T(8,128)(2,1)} %field.1), custom_call_target="tpu_custom_call" | custom-call | tf_op jit(solution)/shard_map/pallas_call | solution.py:189
  12.2 0.5 %collective-permute-start = (bf16[80,640]{1,0:T(8,128)(2,1)S(1)}, bf16[80,640]{1,0:T(8,128)(2,1)S(1)}, u32[]{:S(2)}, u32[]{:S(2)}) collective-permute-start(bf16[80,640]{1,0:T(8,128)(2,1)S(1)} %get-tuple-element.10), channel_id=1, source_target_pairs={{0,1},{1,0},{2,3},{3,2},{4,5},{5,4},{6,7},{7,6},{8,9},{9,8},{10,11... | collective-permute-start | bytes 307208 | tf_op jit(solution)/shard_map/ppermute | solution.py:435
  12.8 2.6 %collective-permute-start.1 = (bf16[80,640]{1,0:T(8,128)(2,1)S(1)}, bf16[80,640]{1,0:T(8,128)(2,1)S(1)}, u32[]{:S(2)}, u32[]{:S(2)}) collective-permute-start(bf16[80,640]{1,0:T(8,128)(2,1)S(1)} %get-tuple-element.11), channel_id=1, source_target_pairs={{0,2},{1,3},{2,0},{3,1},{4,6},{5,7},{6,4},{7,5},{8,10},{9,11},{10,... | collective-permute-start | bytes 307208 | tf_op jit(solution)/shard_map/ppermute | solution.py:435
  15.4 0.1 collective-permute-start.2
  15.4 0.0 collective-permute-done.refs_1_
  15.4 3.7 %collective-permute-done.1.refs_2_ = bf16[80,640]{1,0:T(8,128)(2,1)S(1)} collective-permute-done((bf16[80,640]{1,0:T(8,128)(2,1)S(1)}, bf16[80,640]{1,0:T(8,128)(2,1)S(1)}, u32[]{:S(2)}, u32[]{:S(2)}) %collective-permute-start.1) | collective-permute-done | bytes 102432 | tf_op jit(solution)/shard_map/ppermute | solution.py:435
  19.1 1.7 %collective-permute-done.2.refs_3_ = bf16[80,640]{1,0:T(8,128)(2,1)S(1)} collective-permute-done((bf16[80,640]{1,0:T(8,128)(2,1)S(1)}, bf16[80,640]{1,0:T(8,128)(2,1)S(1)}, u32[]{:S(2)}, u32[]{:S(2)}) %collective-permute-start.2) | collective-permute-done | bytes 102432 | tf_op jit(solution)/shard_map/ppermute | solution.py:435
  20.8 0.0 copy-done.3
  20.8 0.0 copy-done
  20.8 0.0 copy-done.5
  20.8 2.2 %shard_map.83 = bf16[32,16,384]{2,1,0:T(8,128)(2,1)S(1)} custom-call(bf16[80,640]{1,0:T(8,128)(2,1)S(1)} %get-tuple-element.9.refs_0_, bf16[80,640]{1,0:T(8,128)(2,1)S(1)} %collective-permute-done.refs_1_, bf16[80,640]{1,0:T(8,128)(2,1)S(1)} %collective-permute-done.1.refs_2_, bf16[80,640]{1,0:T(8,128)(2,1)S(1)} %collective-permute-done.2.refs_3_, ...), custom_call_target="tpu_custom_call" | custom-call | tf_op jit(solution)/shard_map/pallas_call | solution.py:293
  23.0 18.9 %all_to_all.5.arrived = bf16[32,16,384]{2,1,0:T(8,128)(2,1)S(1)} all-to-all(bf16[32,16,384]{2,1,0:T(8,128)(2,1)S(1)} %shard_map.83), channel_id=1, replica_groups=mesh['rows'=8,'cols'=4] {'rows','cols'}, dimensions={0} | all-to-all | bytes 786432 | tf_op jit(solution)/shard_map/all_to_all | solution.py:437
  41.9 0.0 copy-done.1
  41.9 0.0 copy-done.2
  41.9 0.0 copy-done.4
  41.9 2.8 %shard_map.84 = f32[648,128]{1,0:T(8,128)} custom-call(bf16[32,16,384]{2,1,0:T(8,128)(2,1)S(1)} %all_to_all.5.arrived, f32[9,256]{1,0:T(8,128)S(1)} %copy-done.4, f32[9,512]{1,0:T(8,128)S(1)} %copy-done.3, bf16[256,512]{1,0:T(8,128)(2,1)S(1)} %copy-done.2, bf16[256,512]{1,0:T(8,128)(2,1)S(1)} %copy-done.1), custom_call_target="tpu_custom_call" | custom-call | tf_op jit(solution)/shard_map/pallas_call | solution.py:414
Async XLA Ops:
  0.0 20.8 %copy-start.3 = (f32[9,512]{1,0:T(8,128)S(1)}, f32[9,512]{1,0:T(8,128)}, u32[]{:S(2)}) copy-start(f32[9,512]{1,0:T(8,128)} %constant.13.clone.refs_5_.twiddle) | copy-start | bytes 55300
  0.0 20.8 %copy-start = (bf16[512,512]{1,0:T(8,128)(2,1)S(1)}, bf16[512,512]{1,0:T(8,128)(2,1)}, u32[]{:S(2)}) copy-start(bf16[512,512]{1,0:T(8,128)(2,1)} %constant.14.clone.refs_6_) | copy-start | bytes 1572868
  0.0 20.8 %copy-start.5 = (f32[1,2304]{1,0:T(1,128)S(1)}, f32[1,2304]{1,0:T(1,128)}, u32[]{:S(2)}) copy-start(f32[1,2304]{1,0:T(1,128)} %constant.12.clone.refs_4_) | copy-start | bytes 27652
  0.0 41.9 %copy-start.1 = (bf16[256,512]{1,0:T(8,128)(2,1)S(1)}, bf16[256,512]{1,0:T(8,128)(2,1)}, u32[]{:S(2)}) copy-start(bf16[256,512]{1,0:T(8,128)(2,1)} %constant.17.clone.low_table) | copy-start | bytes 786436
  0.0 41.9 %copy-start.2 = (bf16[256,512]{1,0:T(8,128)(2,1)S(1)}, bf16[256,512]{1,0:T(8,128)(2,1)}, u32[]{:S(2)}) copy-start(bf16[256,512]{1,0:T(8,128)(2,1)} %constant.16.clone.high_table) | copy-start | bytes 786436
  0.0 41.9 %copy-start.4 = (f32[9,256]{1,0:T(8,128)S(1)}, f32[9,256]{1,0:T(8,128)}, u32[]{:S(2)}) copy-start(f32[9,256]{1,0:T(8,128)} %constant.15.clone.weight) | copy-start | bytes 27652
  12.2 3.2 %collective-permute-start = (bf16[80,640]{1,0:T(8,128)(2,1)S(1)}, bf16[80,640]{1,0:T(8,128)(2,1)S(1)}, u32[]{:S(2)}, u32[]{:S(2)}) collective-permute-start(bf16[80,640]{1,0:T(8,128)(2,1)S(1)} %get-tuple-element.10), channel_id=1, source_target_pairs={{0,1},{1,0},{2,3},{3,2},{4,5},{5,4},{6,7},{7,6},{8,9},{9,8},{10,11... | collective-permute-start | bytes 307208 | tf_op jit(solution)/shard_map/ppermute | solution.py:435
  12.8 6.3 %collective-permute-start.1 = (bf16[80,640]{1,0:T(8,128)(2,1)S(1)}, bf16[80,640]{1,0:T(8,128)(2,1)S(1)}, u32[]{:S(2)}, u32[]{:S(2)}) collective-permute-start(bf16[80,640]{1,0:T(8,128)(2,1)S(1)} %get-tuple-element.11), channel_id=1, source_target_pairs={{0,2},{1,3},{2,0},{3,1},{4,6},{5,7},{6,4},{7,5},{8,10},{9,11},{10,... | collective-permute-start | bytes 307208 | tf_op jit(solution)/shard_map/ppermute | solution.py:435
  15.4 5.4 %collective-permute-start.2 = (bf16[80,640]{1,0:T(8,128)(2,1)S(1)}, bf16[80,640]{1,0:T(8,128)(2,1)S(1)}, u32[]{:S(2)}, u32[]{:S(2)}) collective-permute-start(bf16[80,640]{1,0:T(8,128)(2,1)S(1)} %get-tuple-element.12), channel_id=1, source_target_pairs={{0,3},{1,2},{2,1},{3,0},{4,7},{5,6},{6,5},{7,4},{8,11},{9,10},{10,... | collective-permute-start | bytes 307208 | tf_op jit(solution)/shard_map/ppermute | solution.py:435
